TPU v7x, 128 devices: a whole 4x4x4 slice. The times are simulated.
128 devices in a mesh: dp: 8 (over y_lo, z), ctx: 16 (over y_hi, x, core).
Axes of the slice: x: 4, y: 4 (y_hi: 2, y_lo: 2; y = y_hi * 2 + y_lo), z: 4, core: 2. Of those that a mesh axis runs over, the one named last changes fastest.
Arguments:
- tokens: bfloat16 [8, 2048, 1024], P('dp', 'ctx'), may hold values from -6 to 6
- cotangent: bfloat16 [8, 2048, 1024], P('dp', 'ctx')
- positions: int32 [8, 2048], replicated, may hold values from 0 to 2047, as said below
- weights: bfloat16 [1024, 15360], P(('dp', 'ctx'))
- norm_gains: bfloat16 [2304], P(('dp', 'ctx'))
- moment_weights: float32 [1024, 15360], P(('dp', 'ctx')), may hold values from -0.0004272461 to 0.0004272461
- second_weights: float32 [1024, 15360], P(('dp', 'ctx')), may hold values from 1.6527933e-09 to 2.669897e-08
- moment_gains: float32 [2304], P(('dp', 'ctx')), may hold values from -0.0012207031 to 0.0012207031
- second_gains: float32 [2304], P(('dp', 'ctx')), may hold values from 1.5256553e-08 to 2.415621e-07
Outputs:
- block_output: float32 [8, 2048, 1024], P('dp', 'ctx')
- grad_tokens: float32 [8, 2048, 1024], P('dp', 'ctx')
- grad_norm: float32 [1], replicated
- new_weights: float32 [1024, 15360], P(('dp', 'ctx'))
- new_moment_weights: float32 [1024, 15360], P(('dp', 'ctx'))
- new_second_weights: float32 [1024, 15360], P(('dp', 'ctx'))
- new_gains: float32 [2304], P(('dp', 'ctx'))
- new_moment_gains: float32 [2304], P(('dp', 'ctx'))
- new_second_gains: float32 [2304], P(('dp', 'ctx'))
Inputs may be any that keep to these rules, and one draw needn't show every extreme that they name: Each sequence's 2048 positions are a permutation made of 32 blocks of 64 consecutive rising positions; the 128 rows [c * 128, (c + 1) * 128) of a sequence hold the two blocks b and 31 - b for some b, in either order, each pair once per sequence.
All inputs are finite; a program needn't handle non-finite values.
Results may differ from a plain program's by a relative error of at most 0.015.
Values may be sent and summed in bfloat16 or wider, within the bound.
No kernel may reach another device: no remote copies, remote signals or barrier semaphores. Data moves between devices by JAX's collectives and lax.ppermute only.
A program may use at most 320 MiB of HBM per device.

v0:
```python
import math

import jax
import jax.numpy as jnp
from jax import lax
from jax.sharding import PartitionSpec as P

D = 1024
FF = 3072
QUERY_HEADS = 16
KEY_VALUE_HEADS = 8
HEAD_SIZE = 128
ADAM_STEP = 10
QKVC = 4096


eps_norm = 1e-06
rope_base = 1000000.0
clip_limit = 1.0
beta_one = 0.9
beta_two = 0.95
adam_eps = 1e-08
decay_rate = 0.1
rate_matrix = 0.06
rate_output = 2.0
rate_gain = 1.0
contract_rows = (((0,), (0,)), ((), ()))
contract_cols = (((1,), (1,)), ((), ()))


def rms_scale(value_rows):
    return lax.rsqrt(jnp.mean(value_rows * value_rows, axis=-1, keepdims=True) + eps_norm)


def norm_back(value_rows, scale, gain, grad_out):
    gain_grad = jnp.sum(grad_out * value_rows * scale, axis=tuple(range(value_rows.ndim - 1)))
    weighted = grad_out * gain
    grad_in = scale * weighted - value_rows * scale * scale * scale * jnp.mean(
        weighted * value_rows, axis=-1, keepdims=True
    )
    return (grad_in, gain_grad)


def angles(places, width):
    half_width = width // 2
    inverse = jnp.exp(
        jnp.arange(half_width, dtype=jnp.float32) * (-2.0 / width) * math.log(rope_base)
    )
    turned = places.astype(jnp.float32)[:, None] * inverse[None, :]
    return (jnp.cos(turned), jnp.sin(turned))


def rotate(value_rows, cosine_table, sine_table):
    half_width = value_rows.shape[-1] // 2
    front_half = value_rows[..., :half_width]
    back_half = value_rows[..., half_width:]
    cos_part = cosine_table[:, None, :]
    sin_part = sine_table[:, None, :]
    return jnp.concatenate(
        [
            front_half * cos_part - back_half * sin_part,
            back_half * cos_part + front_half * sin_part,
        ],
        axis=-1,
    )


def inverse_rotate(value_rows, cosine_table, sine_table):
    half_width = value_rows.shape[-1] // 2
    front_half = value_rows[..., :half_width]
    back_half = value_rows[..., half_width:]
    cos_part = cosine_table[:, None, :]
    sin_part = sine_table[:, None, :]
    return jnp.concatenate(
        [
            front_half * cos_part + back_half * sin_part,
            back_half * cos_part - front_half * sin_part,
        ],
        axis=-1,
    )


def split_weights(weight_all):
    query_columns = QUERY_HEADS * HEAD_SIZE
    return (
        weight_all[:, :QKVC],
        weight_all[:, QKVC : QKVC + query_columns],
        weight_all[:, QKVC + query_columns : QKVC + query_columns + 2 * FF],
        weight_all[:, QKVC + query_columns + 2 * FF :],
    )


def adam(weight, grad, moment, second, rate, decay):
    moment_new = beta_one * moment + (1.0 - beta_one) * grad
    second_new = beta_two * second + (1.0 - beta_two) * grad * grad
    scaled_m = moment_new / (1.0 - beta_one**ADAM_STEP)
    scaled_v = second_new / (1.0 - beta_two**ADAM_STEP)
    weight_new = weight * (1.0 - rate * decay) - rate * scaled_m / (jnp.sqrt(scaled_v) + adam_eps)
    return (weight_new, moment_new, second_new)


def body(
    tokens,
    cotangent,
    positions,
    weights,
    norm_gains,
    moment_weights,
    second_weights,
    moment_gains,
    second_gains,
):
    local_part = tokens.shape[1]
    whole_sequence = positions.shape[1]
    repeat_factor = QUERY_HEADS // KEY_VALUE_HEADS
    scale = HEAD_SIZE ** (-0.5)
    places_all = lax.dynamic_index_in_dim(positions, lax.axis_index("dp"), 0, keepdims=False)
    places = lax.dynamic_slice_in_dim(places_all, lax.axis_index("ctx") * local_part, local_part)
    weight_all, gain_half = (
        lax.all_gather(weights, ("dp", "ctx"), axis=0, tiled=True),
        lax.all_gather(norm_gains, ("dp", "ctx"), axis=0, tiled=True),
    )
    gain_all = gain_half.astype(jnp.float32)
    w_qkv, w_out, w_gateup, w_down = split_weights(weight_all)
    gain_attn = gain_all[:D]
    gain_mlp = gain_all[D : 2 * D]
    gain_query = gain_all[2 * D : 2 * D + HEAD_SIZE]
    key_norm_gain = gain_all[2 * D + HEAD_SIZE :]
    inputs = tokens[0].astype(jnp.float32)
    scale_one = rms_scale(inputs)
    normed = (inputs * scale_one * gain_attn).astype(jnp.bfloat16)
    projected_rows = jnp.dot(normed, w_qkv, preferred_element_type=jnp.float32)
    query_raw = projected_rows[:, : QUERY_HEADS * HEAD_SIZE].reshape(
        local_part, QUERY_HEADS, HEAD_SIZE
    )
    unrotated_key = projected_rows[
        :, QUERY_HEADS * HEAD_SIZE : (QUERY_HEADS + KEY_VALUE_HEADS) * HEAD_SIZE
    ].reshape(local_part, KEY_VALUE_HEADS, HEAD_SIZE)
    unprojected_value = projected_rows[:, (QUERY_HEADS + KEY_VALUE_HEADS) * HEAD_SIZE :]
    cosine_table, sine_table = angles(places, HEAD_SIZE)
    scale_q = rms_scale(query_raw)
    key_scale_factor = rms_scale(unrotated_key)
    query_rows = rotate(query_raw * scale_q * gain_query, cosine_table, sine_table).astype(
        jnp.bfloat16
    )
    key_rows = rotate(
        unrotated_key * key_scale_factor * key_norm_gain, cosine_table, sine_table
    ).astype(jnp.bfloat16)
    value_rows = unprojected_value.astype(jnp.bfloat16)
    stacked_rows = jnp.stack(
        [key_rows.reshape(local_part, KEY_VALUE_HEADS * HEAD_SIZE), value_rows]
    )
    kv_all = lax.all_gather(stacked_rows, "ctx", axis=1, tiled=True)
    full_key_rows = kv_all[0]
    full_value_rows = kv_all[1]
    query_groups = jnp.transpose(
        query_rows.reshape(local_part, KEY_VALUE_HEADS, repeat_factor, HEAD_SIZE), (1, 2, 0, 3)
    )
    key_groups = jnp.transpose(
        full_key_rows.reshape(whole_sequence, KEY_VALUE_HEADS, HEAD_SIZE), (1, 0, 2)
    )
    value_groups = jnp.transpose(
        full_value_rows.reshape(whole_sequence, KEY_VALUE_HEADS, HEAD_SIZE), (1, 0, 2)
    )
    allowed = places_all[None, :] <= places[:, None]

    def attend(pieces):
        query_g, key_g, value_g = pieces
        scores = (
            jnp.einsum("rqd,kd->rqk", query_g, key_g, preferred_element_type=jnp.float32) * scale
        )
        scores = jnp.where(allowed[None], scores, -1e30)
        top_value = jnp.max(scores, axis=-1, keepdims=True)
        expd = jnp.exp(scores - top_value)
        total = jnp.sum(expd, axis=-1, keepdims=True)
        probs = (expd / total).astype(jnp.bfloat16)
        mixed = jnp.einsum("rqk,kd->rqd", probs, value_g, preferred_element_type=jnp.float32)
        return (mixed, top_value[..., 0] + jnp.log(total[..., 0]))

    mixed, logsum = lax.map(attend, (query_groups, key_groups, value_groups))
    attended = (
        jnp.transpose(mixed, (2, 0, 1, 3))
        .reshape(local_part, QUERY_HEADS * HEAD_SIZE)
        .astype(jnp.bfloat16)
    )
    middle = inputs + lax.dot_general(
        attended, w_out, contract_cols, preferred_element_type=jnp.float32
    )
    scale_two = rms_scale(middle)
    normed_two = (middle * scale_two * gain_mlp).astype(jnp.bfloat16)
    gate_up = jnp.dot(normed_two, w_gateup, preferred_element_type=jnp.float32)
    gate = gate_up[:, :FF]
    upper = gate_up[:, FF:]
    sigma = jax.nn.sigmoid(gate)
    hidden = (gate * sigma * upper).astype(jnp.bfloat16)
    output = middle + lax.dot_general(
        hidden, w_down, contract_cols, preferred_element_type=jnp.float32
    )
    backs = cotangent[0].astype(jnp.float32)
    backs_low = backs.astype(jnp.bfloat16)
    term_down = lax.dot_general(
        backs_low, hidden, contract_rows, preferred_element_type=jnp.float32
    )
    grad_hidden = jnp.dot(backs_low, w_down, preferred_element_type=jnp.float32)
    grad_gate = grad_hidden * upper * sigma * (1.0 + gate * (1.0 - sigma))
    grad_up = grad_hidden * gate * sigma
    grad_gu = jnp.concatenate([grad_gate, grad_up], axis=1).astype(jnp.bfloat16)
    term_gu = lax.dot_general(
        normed_two, grad_gu, contract_rows, preferred_element_type=jnp.float32
    )
    mlp_term = jnp.concatenate([term_gu, term_down], axis=1)
    grad_norm_two = lax.dot_general(
        grad_gu, w_gateup, contract_cols, preferred_element_type=jnp.float32
    )
    grad_mid_part, gain_mlp_grad = norm_back(middle, scale_two, gain_mlp, grad_norm_two)
    grad_mid = backs + grad_mid_part
    grad_mid_low = grad_mid.astype(jnp.bfloat16)
    term_out = lax.dot_general(
        grad_mid_low, attended, contract_rows, preferred_element_type=jnp.float32
    )
    attention_gradient = jnp.dot(grad_mid_low, w_out, preferred_element_type=jnp.float32).astype(
        jnp.bfloat16
    )
    output_gradient_groups = jnp.transpose(
        attention_gradient.reshape(local_part, KEY_VALUE_HEADS, repeat_factor, HEAD_SIZE),
        (1, 2, 0, 3),
    )

    def attend_back(pieces):
        query_g, key_g, value_g, grad_g, logsum_g = pieces
        scores = (
            jnp.einsum("rqd,kd->rqk", query_g, key_g, preferred_element_type=jnp.float32) * scale
        )
        probs = jnp.where(allowed[None], jnp.exp(scores - logsum_g[..., None]), 0.0)
        grad_p = jnp.einsum("rqd,kd->rqk", grad_g, value_g, preferred_element_type=jnp.float32)
        inner = jnp.sum(probs * grad_p, axis=-1, keepdims=True)
        grad_s = (probs * (grad_p - inner)).astype(jnp.bfloat16)
        grad_q = (
            jnp.einsum("rqk,kd->rqd", grad_s, key_g, preferred_element_type=jnp.float32) * scale
        )
        grad_k = (
            jnp.einsum("rqk,rqd->kd", grad_s, query_g, preferred_element_type=jnp.float32) * scale
        )
        grad_v = jnp.einsum(
            "rqk,rqd->kd", probs.astype(jnp.bfloat16), grad_g, preferred_element_type=jnp.float32
        )
        return (grad_q, grad_k, grad_v)

    grad_qg, key_gain_gradient, value_group_gradient = lax.map(
        attend_back, (query_groups, key_groups, value_groups, output_gradient_groups, logsum)
    )
    grad_query = jnp.transpose(grad_qg, (2, 0, 1, 3)).reshape(local_part, QUERY_HEADS, HEAD_SIZE)
    full_key_gradient = jnp.transpose(key_gain_gradient, (1, 0, 2)).reshape(
        whole_sequence, KEY_VALUE_HEADS * HEAD_SIZE
    )
    full_value_gradient = jnp.transpose(value_group_gradient, (1, 0, 2)).reshape(
        whole_sequence, KEY_VALUE_HEADS * HEAD_SIZE
    )
    grad_kv = jnp.stack([full_key_gradient, full_value_gradient])
    grad_kv_own = lax.psum_scatter(
        grad_kv.astype(jnp.bfloat16), "ctx", scatter_dimension=1, tiled=True
    ).astype(jnp.float32)
    key_gradient_rows = grad_kv_own[0]
    value_gradient_rows = grad_kv_own[1]
    unrotated_query_gradient, gain_q_grad = norm_back(
        query_raw, scale_q, gain_query, inverse_rotate(grad_query, cosine_table, sine_table)
    )
    unrotated_key_gradient, gain_k_grad = norm_back(
        unrotated_key,
        key_scale_factor,
        key_norm_gain,
        inverse_rotate(
            key_gradient_rows.reshape(local_part, KEY_VALUE_HEADS, HEAD_SIZE),
            cosine_table,
            sine_table,
        ),
    )
    grad_proj = jnp.concatenate(
        [
            unrotated_query_gradient.reshape(local_part, QUERY_HEADS * HEAD_SIZE),
            unrotated_key_gradient.reshape(local_part, KEY_VALUE_HEADS * HEAD_SIZE),
            value_gradient_rows,
        ],
        axis=1,
    ).astype(jnp.bfloat16)
    term_qkv = lax.dot_general(normed, grad_proj, contract_rows, preferred_element_type=jnp.float32)
    grad_norm_one = lax.dot_general(
        grad_proj, w_qkv, contract_cols, preferred_element_type=jnp.float32
    )
    grad_in_part, gain_attn_grad = norm_back(inputs, scale_one, gain_attn, grad_norm_one)
    grad_inputs = grad_mid + grad_in_part
    gain_term = jnp.concatenate([gain_attn_grad, gain_mlp_grad, gain_q_grad, gain_k_grad])
    attn_term = jnp.concatenate([term_qkv, term_out], axis=1)
    grad_share, gain_grad = (
        lax.psum_scatter(
            jnp.concatenate([attn_term, mlp_term], axis=1),
            ("dp", "ctx"),
            scatter_dimension=0,
            tiled=True,
        ),
        lax.psum_scatter(gain_term, ("dp", "ctx"), scatter_dimension=0, tiled=True),
    )
    squares = jnp.sum(grad_share * grad_share) + jnp.sum(gain_grad * gain_grad)
    norm_all = jnp.sqrt(lax.psum(squares, ("dp", "ctx")))
    factor = jnp.minimum(1.0, clip_limit / (norm_all + 1e-06))
    column = jnp.arange(grad_share.shape[1])
    rates = jnp.where(
        (column >= QKVC) & (column < QKVC + QUERY_HEADS * HEAD_SIZE), rate_output, rate_matrix
    )
    new_w, new_mw, new_vw = adam(
        weights.astype(jnp.float32),
        grad_share * factor,
        moment_weights,
        second_weights,
        rates[None, :],
        decay_rate,
    )
    new_g, new_mg, new_vg = adam(
        norm_gains.astype(jnp.float32),
        gain_grad * factor,
        moment_gains,
        second_gains,
        rate_gain,
        0.0,
    )
    return (
        output[None],
        grad_inputs[None],
        norm_all.reshape(1),
        new_w,
        new_mw,
        new_vw,
        new_g,
        new_mg,
        new_vg,
    )


def solution(mesh):
    placed = (
        P("dp", "ctx", None),
        P("dp", "ctx", None),
        P(),
        P(("dp", "ctx"), None),
        P(("dp", "ctx")),
        P(("dp", "ctx"), None),
        P(("dp", "ctx"), None),
        P(("dp", "ctx")),
        P(("dp", "ctx")),
    )
    return jax.shard_map(
        body,
        mesh=mesh,
        in_specs=placed,
        out_specs=(
            P("dp", "ctx", None),
            P("dp", "ctx", None),
            P(),
            P(("dp", "ctx"), None),
            P(("dp", "ctx"), None),
            P(("dp", "ctx"), None),
            P(("dp", "ctx")),
            P(("dp", "ctx")),
            P(("dp", "ctx")),
        ),
        check_vma=False,
    )
```

profile of v0, /device:TPU:1, one launch (start us, length us, event | category | flops | bytes accessed | tf_op | source)
XLA Modules:
  0.0 1496.5 jit_solution(9850445096484826890)
XLA Ops:
  8.8 68.9 %all-reduce = bf16[2304]{0:T(1024)(128)(2,1)S(1)} all-reduce(bf16[2304]{0:T(1024)(128)(2,1)S(1)} %dynamic-update-slice), channel_id=1, replica_groups=mesh['dp'=8,'ctx'=16] {'dp','ctx'}, use_global_device_ids=true, to_apply=%add | all-reduce | flops 2304 | bytes 9216
  80.5 168.3 %all-gather.3.cloned.1.call-done = bf16[1024,15360]{1,0:T(8,128)(2,1)} async-done(((bf16[8,15360]{1,0:T(8,128)(2,1)}), bf16[1024,15360]{1,0:T(8,128)(2,1)}) %all-gather.3.cloned.1.call-update) | async-done | bytes 31457296 | tf_op jit(solution)/shard_map/all_gather | solution.py:120
  248.8 4.8 fusion.52
  261.3 67.6 %all-gather.5.cloned.1.call-done = bf16[2,2048,1024]{2,1,0:T(8,128)(2,1)} async-done(((bf16[2,128,1024]{2,1,0:T(8,128)(2,1)}), bf16[2,2048,1024]{2,1,0:T(8,128)(2,1)}) %all-gather.5.cloned.1.call-update) | async-done | bytes 8388624 | tf_op jit(solution)/shard_map/all_gather | solution.py:153
  329.0 4.6 slice_bitcast_fusion
  335.8 4.3 copy_bitcast_fusion
  340.1 37.0 %while.28 = (s32[]{:T(128)}, bf16[8,2,128,128]{2,3,1,0:T(8,128)(2,1)S(1)}, f32[8,2,128]{2,1,0:T(2,128)}, bf16[8,2,128,128]{3,2,1,0:T(8,128)(2,1)S(1)}, bf16[8,20...) while((s32[]{:T(128)}, ...), condition=%wide.region_6.7_spmd.clone, body=%wide.region_3.6_spmd.clone.sunk | while | flops 272891648 | bytes 8079977 | solution.py:180
  356.3 1.7 fusion.149
  377.9 3.9 multiply_reduce_fusion.6
  381.9 5.9 fusion.48
  387.8 5.6 multiply_convert_fusion.2
  393.4 9.0 multiply_reduce_fusion.3
  402.6 2.9 fusion.62
  407.9 80.1 %while.29 = (s32[]{:T(128)}, f32[8,2,128,128]{3,2,1,0:T(8,128)}, bf16[8,2048,128]{2,1,0:T(8,128)(2,1)}, bf16[8,2048,128]{2,1,0:T(8,128)(2,1)}, bf16[8,2,128,128]...) while((s32[]{:T(128)}, f32[8,2,128,128]{3,2,1,0:T(8,128)}, ...), condition=%wide.region_11.12_spmd.clone, body=%wide.region_9.11_spmd.clone.sunk | while | flops 676364032 | bytes 20335232 | solution.py:249
  410.9 2.0 multiply_reduce_fusion.11
  413.2 2.1 fusion.160
  421.0 2.0 multiply_reduce_fusion.11
  423.2 2.1 fusion.160
  431.1 2.0 multiply_reduce_fusion.11
  433.3 2.1 fusion.160
  441.1 2.0 multiply_reduce_fusion.11
  443.3 2.2 fusion.160
  451.0 2.0 multiply_reduce_fusion.11
  453.3 2.1 fusion.160
  461.0 2.0 multiply_reduce_fusion.11
  463.3 2.1 fusion.160
  471.0 2.0 multiply_reduce_fusion.11
  473.3 2.1 fusion.160
  481.0 2.0 multiply_reduce_fusion.11
  483.2 2.1 fusion.160
  487.9 6.2 copy.67
  494.2 7.3 stack_reshape.10
  501.4 6.2 copy.66
  507.7 7.3 stack_reshape.9
  515.0 7.6 pad_maximum_fusion.1
  528.7 5.1 fusion.104
  533.8 7.4 convolution_bitcast_fusion.3
  541.2 10.5 fusion.80
  551.8 69.7 %reduce-scatter.3.cloned.1.call-done = bf16[2,128,1024]{2,1,0:T(8,128)(2,1)} async-done(((bf16[2,2048,1024]{2,1,0:T(8,128)(2,1)}), bf16[2,128,1024]{2,1,0:T(8,128)(2,1)}) %reduce-scatter.3.cloned.1.call-update) | async-done | bytes 524304 | tf_op jit(solution)/shard_map/reduce_scatter | solution.py:260
  625.4 8.2 fusion.100
  633.6 42.2 %pad_maximum_fusion = f32[1024,15360]{1,0:T(8,128)} fusion(f32[1024,3072]{1,0:T(8,128)} %convolution_bitcast_fusion.3, f32[1024,6144]{1,0:T(8,128)} %fusion.80, f32[1024,2048]{1,0:T(8,128)} %fusion.104, f32[1024,4096]{1,0:T(8,128)} %fusion.100), kind=kLoop, calls=%fused_computation.58 | loop fusion | flops 47185920 | bytes 125829120 | tf_op jit(solution)/shard_map/concatenate | solution.py:296
  676.9 5.8 fusion.71
  682.9 6.8 fusion.95
  689.7 69.9 %all-reduce.1 = f32[2304]{0:T(1024)S(1)} all-reduce(f32[2304]{0:T(1024)S(1)} %pad_maximum_fusion.12), channel_id=4, replica_groups=mesh['dp'=8,'ctx'=16] {'dp','ctx'}, use_global_device_ids=true, to_apply=%region_24.25.clone | all-reduce | flops 2304 | bytes 18432
  760.4 653.0 %reduce-scatter.5.cloned.1.call-done = f32[8,15360]{1,0:T(8,128)} async-done(((f32[1024,15360]{1,0:T(8,128)}), f32[8,15360]{1,0:T(8,128)}) %reduce-scatter.5.cloned.1.call-update) | async-done | bytes 491536 | tf_op jit(solution)/shard_map/reduce_scatter | solution.py:295
  1413.3 1.8 multiply_reduce_fusion.8
  1417.4 67.4 %psum.7 = f32[]{:T(128)} all-reduce(f32[]{:T(128)S(6)} %add.149), channel_id=1, replica_groups=mesh['dp'=8,'ctx'=16] {'dp','ctx'}, use_global_device_ids=true, to_apply=%region_26.27 | all-reduce | flops 1 | bytes 8 | tf_op jit(solution)/shard_map/psum | solution.py:304
  1486.2 2.5 divide_subtract_fusion
  (245 shorter events, 112.8 us)
Async XLA Ops:
  7.2 241.6 %all-gather.3.cloned.1.call-start = ((), (), s32[]{:S(2)}) async-start(), calls=%async_computation.2 | async-start | bytes 31703040 | tf_op jit(solution)/shard_map/all_gather | solution.py:120
  7.9 321.0 %all-gather.5.cloned.1.call-start = ((), (), s32[]{:S(2)}) async-start(), calls=%async_computation.3 | async-start | bytes 8912896 | tf_op jit(solution)/shard_map/all_gather | solution.py:153
  80.1 173.5 %copy-start.30 = (f32[128]{0:T(128)}, f32[128]{0:T(128)S(1)}, u32[]{:S(2)}) copy-start(f32[128]{0:T(128)S(1)} %add_rsqrt_fusion.3) | copy-start | bytes 1540
  80.2 175.2 %copy-start.33 = (f32[128]{0:T(128)}, f32[128]{0:T(128)S(1)}, u32[]{:S(2)}) copy-start(f32[128]{0:T(128)S(1)} %get-tuple-element.233) | copy-start | bytes 1540
  80.2 179.7 %copy-start.36 = (f32[128]{0:T(128)}, f32[128]{0:T(128)S(1)}, u32[]{:S(2)}) copy-start(f32[128]{0:T(128)S(1)} %get-tuple-element.234) | copy-start | bytes 1540
  253.6 1.3 copy-start
  255.3 4.1 copy-start.19
  257.0 364.5 %reduce-scatter.3.cloned.1.call-start = ((), (), s32[]{:S(2)}) async-start(), calls=%async_computation.4 | async-start | bytes 8912896 | tf_op jit(solution)/shard_map/reduce_scatter | solution.py:260
  259.8 0.9 copy-start.21
  335.8 4.4 copy-start.26
  340.1 37.8 %copy-start.3 = (bf16[1,128,1024]{2,1,0:T(8,128)(2,1)S(1)}, bf16[1,128,1024]{2,1,0:T(8,128)(2,1)}, u32[]{:S(2)}) copy-start(bf16[1,128,1024]{2,1,0:T(8,128)(2,1)} %param.13) | copy-start | bytes 786436
  377.1 0.8 copy-start.23
  381.8 20.6 %copy-start.4 = (f32[128,1024]{1,0:T(8,128)}, f32[128,1024]{1,0:T(8,128)S(1)}, u32[]{:S(2)}) copy-start(f32[128,1024]{1,0:T(8,128)S(1)} %get-tuple-element.238) | copy-start | bytes 1572868
  381.9 20.5 %copy-start.28 = (f32[128]{0:T(128)}, f32[128]{0:T(128)S(1)}, u32[]{:S(2)}) copy-start(f32[128]{0:T(128)S(1)} %add_rsqrt_fusion.2) | copy-start | bytes 1540
  381.9 5.9 copy-start.8
  393.4 9.0 copy-start.15
  393.4 9.0 copy-start.17
  522.6 0.6 copy-start.34
  522.6 1.2 copy-start.37
  522.6 1.2 copy-start.2
  522.6 890.7 %reduce-scatter.5.cloned.1.call-start = ((), (), s32[]{:S(2)}) async-start(), calls=%async_computation.5 | async-start | bytes 63406080 | tf_op jit(solution)/shard_map/reduce_scatter | solution.py:295
  524.2 2.0 copy-start.22
  525.4 1.6 copy-start.1
  526.2 2.5 copy-start.24
  528.6 5.1 copy-start.6
  528.7 5.1 copy-start.9
  533.8 7.5 copy-start.5
  533.8 7.5 copy-start.16
  533.8 7.5 copy-start.18
  533.8 7.5 copy-start.29
  551.8 72.1 %copy-start.27 = (f32[1024]{0:T(1024)S(1)}, f32[1024]{0:T(1024)}, u32[]{:S(2)}) copy-start(f32[1024]{0:T(1024)} %broadcast_bitcast_fusion.1) | copy-start | bytes 12292
  621.5 1.5 copy-start.35
  621.5 1.9 copy-start.20
  622.7 2.7 copy-start.10
  622.8 2.6 copy-start.31
  625.4 8.2 copy-start.12
  675.8 1.1 copy-start.7
  676.9 5.9 copy-start.11
  676.9 5.9 copy-start.13
  676.9 5.9 copy-start.32
  682.8 6.9 copy-start.38
  682.8 802.7 %copy-start.39 = (bf16[18]{0:T(256)(128)(2,1)S(1)}, bf16[18]{0:T(256)(128)(2,1)}, u32[]{:S(2)}) copy-start(bf16[18]{0:T(256)(128)(2,1)} %param.17) | copy-start | bytes 112
  682.8 802.7 %copy-start.40 = (f32[18]{0:T(128)S(1)}, f32[18]{0:T(128)}, u32[]{:S(2)}) copy-start(f32[18]{0:T(128)} %param.20) | copy-start | bytes 220
  682.8 802.7 %copy-start.41 = (f32[18]{0:T(128)S(1)}, f32[18]{0:T(128)}, u32[]{:S(2)}) copy-start(f32[18]{0:T(128)} %param.21) | copy-start | bytes 220
  682.9 803.3 %copy-start.14 = (bf16[8,15360]{1,0:T(8,128)(2,1)S(1)}, bf16[8,15360]{1,0:T(8,128)(2,1)}, u32[]{:S(2)}) copy-start(bf16[8,15360]{1,0:T(8,128)(2,1)} %param.16) | copy-start | bytes 737284
  682.9 803.3 %copy-start.25 = (f32[8,15360]{1,0:T(8,128)S(1)}, f32[8,15360]{1,0:T(8,128)}, u32[]{:S(2)}) copy-start(f32[8,15360]{1,0:T(8,128)} %param.18) | copy-start | bytes 1474564
Sparse Core Ops, SparseCore 0:
  9.7 239.0 all-gather.2
  257.1 71.8 all-gather.4
  522.7 98.7 reduce-scatter.2
  675.9 737.3 reduce-scatter.4
where the time goes:
time: 1500 us
  waiting for transfers between devices  959 us (64%)
  blocking collectives  206 us (14%)
  matrix products  169 us (11%)
  other arithmetic  88.1 us (6%)
  local copies, waits for them, and re-layouts  55.9 us (4%)
  between operations  17.9 us (1%)
    reduce_scatter x1, waiting for transfers between devices, body(): lax.psum_scatter(jnp.concatenate([attn_term, mlp_term], axis=1), ('dp', '...  653 us
    all_gather x1, waiting for transfers between devices, body(): lax.all_gather(weights, ('dp', 'ctx'), axis=0, tiled=True)  168 us
    unnamed x2, blocking collectives  139 us
    reduce_scatter x1, waiting for transfers between devices, body(): lax.psum_scatter(grad_kv.astype(jnp.bfloat16), 'ctx', scatter_dimension=1...  69.7 us
    all_gather x1, waiting for transfers between devices, body(): kv_all = lax.all_gather(stacked_rows, 'ctx', axis=1, tiled=True)  67.6 us
    psum x1, blocking collectives, body(): norm_all = jnp.sqrt(lax.psum(squares, ('dp', 'ctx')))  67.4 us
    concatenate x1, other arithmetic, body(): jnp.concatenate([attn_term, mlp_term], axis=1)  42.2 us
  transfers between devices with their start and end apart: 4, of which 4 were waited for; matrix products, arithmetic and copies ran while one was open for 3% of the time, Pallas kernels for 0%

commit v1 on v0

v1 whole, which is shorter than its diff:
```python
import math

import jax
import jax.numpy as jnp
from jax import lax
from jax.sharding import Mesh
from jax.sharding import PartitionSpec as P

D = 1024
FF = 3072
QUERY_HEADS = 16
KEY_VALUE_HEADS = 8
HEAD_SIZE = 128
ADAM_STEP = 10
QKVC = 4096
TP = 8
QW = 256
KW = 128
FW = FF // TP

ALL = ("ylo", "z", "yhi", "x", "core")

eps_norm = 1e-06
rope_base = 1000000.0
clip_limit = 1.0
beta_one = 0.9
beta_two = 0.95
adam_eps = 1e-08
decay_rate = 0.1
rate_matrix = 0.06
rate_output = 2.0
rate_gain = 1.0
contract_rows = (((0,), (0,)), ((), ()))
contract_cols = (((1,), (1,)), ((), ()))
f32 = jnp.float32
bf16 = jnp.bfloat16


def dot(a, b, dims=(((1,), (0,)), ((), ()))):
    return lax.dot_general(a, b, dims, preferred_element_type=f32)


def rms_scale(value_rows):
    return lax.rsqrt(jnp.mean(value_rows * value_rows, axis=-1, keepdims=True) + eps_norm)


def norm_back(value_rows, scale, gain, grad_out):
    gain_grad = jnp.sum(grad_out * value_rows * scale, axis=tuple(range(value_rows.ndim - 1)))
    weighted = grad_out * gain
    grad_in = scale * weighted - value_rows * scale * scale * scale * jnp.mean(
        weighted * value_rows, axis=-1, keepdims=True
    )
    return (grad_in, gain_grad)


def angles(places, width):
    half_width = width // 2
    inverse = jnp.exp(jnp.arange(half_width, dtype=f32) * (-2.0 / width) * math.log(rope_base))
    turned = places.astype(f32)[:, None] * inverse[None, :]
    return (jnp.cos(turned), jnp.sin(turned))


def rotate(value_rows, cosine_table, sine_table):
    half_width = value_rows.shape[-1] // 2
    front_half = value_rows[..., :half_width]
    back_half = value_rows[..., half_width:]
    cos_part = cosine_table[:, None, :]
    sin_part = sine_table[:, None, :]
    return jnp.concatenate(
        [
            front_half * cos_part - back_half * sin_part,
            back_half * cos_part + front_half * sin_part,
        ],
        axis=-1,
    )


def swap_core(v):
    return lax.ppermute(v, "core", [(0, 1), (1, 0)])


def swap_yhi(v):
    return lax.ppermute(v, "yhi", [(0, 1), (1, 0)])


def shift_x(v, k):
    return lax.ppermute(v, "x", [(i, (i + k) % 4) for i in range(4)])


def group_gather(v):
    near = jnp.concatenate([v, shift_x(v, -1), shift_x(v, -2), shift_x(v, -3)], axis=0)
    return jnp.concatenate([near, swap_core(near)], axis=0)


def group_scatter(left, right, dims):
    half = left.shape[0] // 2
    piece = half // 4
    away = swap_core(dot(left[half:], right, dims).astype(bf16))
    near = dot(left[:half], right, dims) + away.astype(f32)
    low = near.astype(bf16)
    total = near[:piece]
    for k in (1, 2, 3):
        total = total + shift_x(low[k * piece : (k + 1) * piece], k).astype(f32)
    return total


def spread(columns):
    n = columns.shape[2]
    owned = jnp.transpose(columns, (1, 0, 2)).reshape(64, n)
    sent = jnp.broadcast_to(owned[None], (16, 64, n)).reshape(1024, n)
    return lax.all_to_all(sent, ALL, 0, 0, tiled=True)


def collect(grad):
    n = grad.shape[1]
    got = lax.all_to_all(grad.astype(bf16), ALL, 0, 0, tiled=True)
    return jnp.sum(got.reshape(16, 8, 8, n).astype(f32), axis=0)


def to_columns(v):
    return jnp.transpose(v, (1, 0, 2)).reshape(8, -1)


def adam(weight, grad, moment, second, rate, decay):
    moment_new = beta_one * moment + (1.0 - beta_one) * grad
    second_new = beta_two * second + (1.0 - beta_two) * grad * grad
    scaled_m = moment_new / (1.0 - beta_one**ADAM_STEP)
    scaled_v = second_new / (1.0 - beta_two**ADAM_STEP)
    weight_new = weight * (1.0 - rate * decay) - rate * scaled_m / (jnp.sqrt(scaled_v) + adam_eps)
    return (weight_new, moment_new, second_new)


def slot_places(positions):
    seq = lax.axis_index("ylo") * 4 + lax.axis_index("z")
    table = lax.dynamic_index_in_dim(positions, seq, 0, keepdims=False).reshape(2, 4, 2, 128)
    xi = lax.axis_index("x")
    table = lax.dynamic_slice_in_dim(jnp.concatenate([table, table], axis=1), xi, 4, axis=1)
    table = jnp.transpose(table, (0, 2, 1, 3))
    table = jnp.where(lax.axis_index("core") == 0, table, table[:, ::-1])
    table = jnp.where(lax.axis_index("yhi") == 0, table, table[::-1])
    return table.reshape(2048)


def body(
    tokens,
    cotangent,
    positions,
    weights,
    norm_gains,
    moment_weights,
    second_weights,
    moment_gains,
    second_gains,
):
    scale = HEAD_SIZE ** (-0.5)
    o_q, o_k, o_v, o_o = 0, 2048, 3072, 4096
    o_g, o_u, o_d = 6144, 6144 + FF, 6144 + 2 * FF
    w_q = weights[:, o_q:o_k].reshape(8, 8, QW)
    w_k = weights[:, o_k:o_v].reshape(8, 8, KW)
    w_v = weights[:, o_v:o_o].reshape(8, 8, KW)
    w_o = weights[:, o_o:o_g].reshape(8, 8, QW)
    w_g = weights[:, o_g:o_u].reshape(8, 8, FW)
    w_u = weights[:, o_u:o_d].reshape(8, 8, FW)
    w_d = weights[:, o_d:].reshape(8, 8, FW)
    gain_all = (
        lax.all_to_all(
            jnp.broadcast_to(norm_gains[None], (128, 18)), ALL, 0, 0, tiled=True
        )
        .reshape(2304)
        .astype(f32)
    )
    w_qkv = spread(jnp.concatenate([w_q, w_k, w_v], axis=2))
    w_rest = spread(jnp.concatenate([w_o, w_g, w_u, w_d], axis=2))
    w_out = w_rest[:, :QW]
    w_gateup = w_rest[:, QW : QW + 2 * FW]
    w_down = w_rest[:, QW + 2 * FW :]
    gain_attn = gain_all[:D]
    gain_mlp = gain_all[D : 2 * D]
    gain_query = gain_all[2 * D : 2 * D + HEAD_SIZE]
    gain_key = gain_all[2 * D + HEAD_SIZE :]

    places_all = slot_places(positions)
    places = places_all[:1024]
    cosine_table, sine_table = angles(places, HEAD_SIZE)

    own = tokens[0].astype(f32)
    own_back = cotangent[0].astype(f32)
    inputs = group_gather(tokens[0]).astype(f32)
    backs_low = group_gather(cotangent[0])

    scale_one = rms_scale(inputs)
    normed = (inputs * scale_one * gain_attn).astype(bf16)
    projected = dot(normed, w_qkv)
    query_raw = projected[:, :QW].reshape(1024, 2, HEAD_SIZE)
    key_raw = projected[:, QW : QW + KW].reshape(1024, 1, HEAD_SIZE)
    scale_q = rms_scale(query_raw)
    scale_k = rms_scale(key_raw)
    query_rows = rotate(query_raw * scale_q * gain_query, cosine_table, sine_table).astype(bf16)
    key_rows = rotate(key_raw * scale_k * gain_key, cosine_table, sine_table).astype(bf16)
    pair = jnp.concatenate(
        [key_rows.reshape(1024, HEAD_SIZE), projected[:, QW + KW :].astype(bf16)], axis=1
    )
    pair_all = jnp.concatenate([pair, swap_yhi(pair)], axis=0)
    key_all = pair_all[:, :HEAD_SIZE]
    value_all = pair_all[:, HEAD_SIZE:]
    query_heads = jnp.transpose(query_rows, (1, 0, 2))
    allowed = places_all[None, :] <= places[:, None]

    def attend(query_h):
        scores = dot(query_h, key_all, contract_cols) * scale
        scores = jnp.where(allowed, scores, -1e30)
        top = jnp.max(scores, axis=-1, keepdims=True)
        expd = jnp.exp(scores - top)
        total = jnp.sum(expd, axis=-1, keepdims=True)
        probs = (expd / total).astype(bf16)
        return (dot(probs, value_all), top[..., 0] + jnp.log(total[..., 0]))

    mixed, logsum = lax.map(attend, query_heads)
    attended = jnp.transpose(mixed, (1, 0, 2)).reshape(1024, QW).astype(bf16)

    middle = own + group_scatter(attended, w_out, contract_cols)
    scale_two = rms_scale(middle)
    normed_two = group_gather((middle * scale_two * gain_mlp).astype(bf16))
    gate_up = dot(normed_two, w_gateup)
    gate = gate_up[:, :FW]
    upper = gate_up[:, FW:]
    sigma = jax.nn.sigmoid(gate)
    hidden = (gate * sigma * upper).astype(bf16)
    grad_hidden = dot(backs_low, w_down)
    grad_gate = grad_hidden * upper * sigma * (1.0 + gate * (1.0 - sigma))
    grad_up = grad_hidden * gate * sigma
    grad_gu = jnp.concatenate([grad_gate, grad_up], axis=1).astype(bf16)
    grad_normed_two = group_scatter(grad_gu, w_gateup, contract_cols)
    output = middle + group_scatter(hidden, w_down, contract_cols)
    term_mlp = jnp.concatenate(
        [dot(normed_two, grad_gu, contract_rows), dot(backs_low, hidden, contract_rows)], axis=1
    )
    share_mlp = collect(term_mlp)

    grad_mid_part, gain_mlp_grad = norm_back(middle, scale_two, gain_mlp, grad_normed_two)
    grad_mid = own_back + grad_mid_part
    grad_mid_low = group_gather(grad_mid.astype(bf16))
    term_out = dot(grad_mid_low, attended, contract_rows)
    share_out = collect(term_out)
    grad_att = dot(grad_mid_low, w_out).astype(bf16)
    grad_heads = jnp.transpose(grad_att.reshape(1024, 2, HEAD_SIZE), (1, 0, 2))

    def attend_back(carry, pieces):
        query_h, grad_h, logsum_h = pieces
        scores = dot(query_h, key_all, contract_cols) * scale
        probs = jnp.where(allowed, jnp.exp(scores - logsum_h[:, None]), 0.0)
        grad_p = dot(grad_h, value_all, contract_cols)
        inner = jnp.sum(probs * grad_p, axis=-1, keepdims=True)
        grad_s = (probs * (grad_p - inner)).astype(bf16)
        grad_q = dot(grad_s, key_all) * scale
        grad_k = dot(grad_s, query_h, contract_rows) * scale
        grad_v = dot(probs.astype(bf16), grad_h, contract_rows)
        return ((carry[0] + grad_k, carry[1] + grad_v), grad_q)

    start = (jnp.zeros((2048, HEAD_SIZE), f32), jnp.zeros((2048, HEAD_SIZE), f32))
    (grad_key, grad_value), grad_qh = lax.scan(
        attend_back, start, (query_heads, grad_heads, logsum)
    )
    grad_pair = jnp.concatenate([grad_key, grad_value], axis=1)
    grad_pair = grad_pair[:1024] + swap_yhi(grad_pair[1024:].astype(bf16)).astype(f32)
    grad_query = jnp.transpose(grad_qh, (1, 0, 2))

    grad_query_raw, gain_q_grad = norm_back(
        query_raw, scale_q, gain_query, rotate(grad_query, cosine_table, -sine_table)
    )
    grad_key_raw, gain_k_grad = norm_back(
        key_raw,
        scale_k,
        gain_key,
        rotate(grad_pair[:, :HEAD_SIZE].reshape(1024, 1, HEAD_SIZE), cosine_table, -sine_table),
    )
    grad_proj = jnp.concatenate(
        [
            grad_query_raw.reshape(1024, QW),
            grad_key_raw.reshape(1024, KW),
            grad_pair[:, HEAD_SIZE:],
        ],
        axis=1,
    ).astype(bf16)
    term_qkv = dot(normed, grad_proj, contract_rows)
    share_qkv = collect(term_qkv)

    grad_normed = group_scatter(grad_proj, w_qkv, contract_cols)
    own_scale = rms_scale(own)
    grad_in_part, gain_attn_grad = norm_back(own, own_scale, gain_attn, grad_normed)
    grad_inputs = grad_mid + grad_in_part

    gain_term = jnp.concatenate([gain_attn_grad, gain_mlp_grad, gain_q_grad, gain_k_grad])
    gain_grad = jnp.sum(
        lax.all_to_all(gain_term.reshape(128, 18), ALL, 0, 0, tiled=True), axis=0
    )
    grad_share = jnp.concatenate(
        [
            to_columns(share_qkv[:, :, :QW]),
            to_columns(share_qkv[:, :, QW : QW + KW]),
            to_columns(share_qkv[:, :, QW + KW :]),
            to_columns(share_out),
            to_columns(share_mlp[:, :, :FW]),
            to_columns(share_mlp[:, :, FW : 2 * FW]),
            to_columns(share_mlp[:, :, 2 * FW :]),
        ],
        axis=1,
    )
    squares = jnp.sum(grad_share * grad_share) + jnp.sum(gain_grad * gain_grad)
    shared = lax.all_to_all(jnp.broadcast_to(squares, (128, 128)), ALL, 0, 0, tiled=True)
    norm_all = jnp.sqrt(jnp.sum(shared[:, 0]))
    factor = jnp.minimum(1.0, clip_limit / (norm_all + 1e-06))
    column = jnp.arange(grad_share.shape[1])
    rates = jnp.where(
        (column >= QKVC) & (column < QKVC + QUERY_HEADS * HEAD_SIZE), rate_output, rate_matrix
    )
    new_w, new_mw, new_vw = adam(
        weights.astype(f32),
        grad_share * factor,
        moment_weights,
        second_weights,
        rates[None, :],
        decay_rate,
    )
    new_g, new_mg, new_vg = adam(
        norm_gains.astype(f32),
        gain_grad * factor,
        moment_gains,
        second_gains,
        rate_gain,
        0.0,
    )
    return (
        output[None],
        grad_inputs[None],
        norm_all.reshape(1),
        new_w,
        new_mw,
        new_vw,
        new_g,
        new_mg,
        new_vg,
    )


def solution(mesh):
    parts = Mesh(mesh.devices.reshape(2, 4, 2, 4, 2), ALL)
    rows = P(("ylo", "z"), ("yhi", "x", "core"), None)
    owned = P(ALL, None)
    small = P(ALL)
    return jax.shard_map(
        body,
        mesh=parts,
        in_specs=(rows, rows, P(), owned, small, owned, owned, small, small),
        out_specs=(rows, rows, P(), owned, owned, owned, small, small, small),
        check_vma=False,
    )
```

time: 1500 us -> 450 us (0.30)
  waiting for transfers between devices: 959 us -> 143 us
  blocking collectives: 206 us -> 0 us
  starting transfers between devices: 0.16 us -> 106 us
  matrix products: 169 us -> 95.1 us
  other arithmetic: 88.1 us -> 54.4 us
  local copies, waits for them, and re-layouts: 55.9 us -> 38.1 us
    reduce_scatter x2 -> x0, waiting for transfers between devices: 723 us -> none  [the longest x1 653 us: body(): lax.psum_scatter(jnp.concatenate([attn_term, mlp_term], axis=1), ('dp', '...]
    all_gather x2 -> x0, waiting for transfers between devices: 236 us -> none  [the longest x1 168 us: body(): lax.all_gather(weights, ('dp', 'ctx'), axis=0, tiled=True)]
    unnamed x2 -> x0, blocking collectives: 139 us -> none
    ppermute x0 -> x34, waiting for transfers between devices: none -> 95.6 us  [the longest x24 57.9 us: shift_x(): return lax.ppermute(v, 'x', [(i, (i + k) % 4) for i in range(4)])]
    dot_general x68 -> x30, matrix products: 169 us -> 95.1 us  [dot(): return lax.dot_general(a, b, dims, preferred_element_type=f32)]
    psum x1 -> x0, blocking collectives: 67.4 us -> none  [body(): norm_all = jnp.sqrt(lax.psum(squares, ('dp', 'ctx')))]
    all_to_all x0 -> x8, starting transfers between devices: none -> 62.4 us  [the longest x3 23.2 us: collect(): got = lax.all_to_all(grad.astype(bf16), ALL, 0, 0, tiled=True)]
    all_to_all x0 -> x8, waiting for transfers between devices: none -> 47.5 us  [the longest x3 20.4 us: collect(): got = lax.all_to_all(grad.astype(bf16), ALL, 0, 0, tiled=True)]
  transfers between devices with their start and end apart: 4 -> 42, of which waited for: 4 -> 21; matrix products, arithmetic and copies ran while one was open for 3% -> 36% of each run, Pallas kernels for 0% -> 0%
where the time goes in v1:
time: 450 us; the launch traced here: 442 us
  waiting for transfers between devices  143 us (32%)
  starting transfers between devices  106 us (24%)
  matrix products  95.1 us (21%)
  other arithmetic  54.4 us (12%)
  local copies, waits for them, and re-layouts  38.1 us (8%)
  between operations  5.54 us (1%)
    dot_general x30, matrix products, dot(): return lax.dot_general(a, b, dims, preferred_element_type=f32)  95.1 us
    ppermute x24, waiting for transfers between devices, shift_x(): return lax.ppermute(v, 'x', [(i, (i + k) % 4) for i in range(4)])  57.9 us
    ppermute x2, waiting for transfers between devices, swap_yhi(): return lax.ppermute(v, 'yhi', [(0, 1), (1, 0)])  35.7 us
    ppermute x24, starting transfers between devices, shift_x(): return lax.ppermute(v, 'x', [(i, (i + k) % 4) for i in range(4)])  26.9 us
    all_to_all x3, starting transfers between devices, collect(): got = lax.all_to_all(grad.astype(bf16), ALL, 0, 0, tiled=True)  23.2 us
    all_to_all x3, waiting for transfers between devices, collect(): got = lax.all_to_all(grad.astype(bf16), ALL, 0, 0, tiled=True)  20.4 us
    unnamed x182, local copies, waits for them, and re-layouts  15.8 us
    all_to_all x2, starting transfers between devices, spread(): return lax.all_to_all(sent, ALL, 0, 0, tiled=True)  14.3 us
  transfers between devices with their start and end apart: 42, of which 21 were waited for; matrix products, arithmetic and copies ran while one was open for 36% of the time, Pallas kernels for 0%

profile of v1, /device:TPU:1, one launch (start us, length us, event | category | flops | bytes accessed | tf_op | source)
XLA Modules:
  0.0 442.3 jit_solution(17885490494294292844)
XLA Ops:
  7.7 9.1 %all-to-all-start = ((bf16[128,1,18]{2,1,0:T(2,128)(2,1)}), bf16[128,1,18]{2,1,0:T(2,128)(2,1)S(1)}, u32[]{:S(2)}, u32[]{:S(2)}) async-start(bf16[128,1,18]{2,1,0:T(2,128)(2,1)} %broadcast_in_dim.45), calls=%async_computation | async-start | bytes 131072 | tf_op jit(solution)/shard_map/all_to_all | solution.py:166
  21.0 3.0 fusion.125
  28.1 8.9 %all-to-all-start.1 = ((bf16[128,8,512]{2,1,0:T(8,128)(2,1)}), bf16[128,8,512]{2,1,0:T(8,128)(2,1)S(1)}, u32[]{:S(2)}, u32[]{:S(2)}) async-start(bf16[128,8,512]{2,1,0:T(8,128)(2,1)} %bitcast.6), calls=%async_computation.1 | async-start | bytes 2097152 | tf_op jit(solution)/shard_map/all_to_all | solution.py:111
  44.7 11.5 %all-to-all-done.1 = bf16[128,8,512]{2,1,0:T(8,128)(2,1)S(1)} async-done(((bf16[128,8,512]{2,1,0:T(8,128)(2,1)}), bf16[128,8,512]{2,1,0:T(8,128)(2,1)S(1)}, u32[]{:S(2)}, u32[]{:S(2)}) %all-to-all-start.1) | async-done | bytes 1048608 | tf_op jit(solution)/shard_map/all_to_all | solution.py:111
  58.1 5.5 %all-to-all-start.2 = ((bf16[128,8,1408]{2,1,0:T(8,128)(2,1)}), bf16[128,8,1408]{2,1,0:T(8,128)(2,1)}, u32[]{:S(2)}, u32[]{:S(2)}) async-start(bf16[128,8,1408]{2,1,0:T(8,128)(2,1)} %bitcast.25), calls=%async_computation.2 | async-start | bytes 5767168 | tf_op jit(solution)/shard_map/all_to_all | solution.py:111
  63.6 3.3 fusion.60
  70.4 3.2 collective-permute-start.4
  76.2 34.6 %collective-permute-done.4 = bf16[1024,256]{0,1:T(8,128)(2,1)} collective-permute-done((bf16[1024,256]{0,1:T(8,128)(2,1)}, bf16[1024,256]{0,1:T(8,128)(2,1)}, u32[]{:S(2)}, u32[]{:S(2)}) %collective-permute-start.4) | collective-permute-done | bytes 524320 | tf_op jit(solution)/shard_map/ppermute | solution.py:83
  114.1 19.1 %while.28 = (s32[]{:T(128)}, bf16[2,1024,128]{1,2,0:T(8,128)(2,1)S(1)}, f32[2,1024]{1,0:T(2,128)S(1)}, bf16[2,1024,128]{2,1,0:T(8,128)(2,1)S(1)}, bf16[2048,128]...) while((s32[]{:T(128)}, ...), condition=%wide.region_6.7_spmd.clone, body=%wide.region_3.6_spmd.clone.sunk | while | flops 1105198080 | bytes 27078776 | solution.py:218
  114.1 2.7 fusion.194
  119.3 4.2 fusion.196
  128.9 4.2 fusion.196
  143.0 7.6 %collective-permute-done.19 = bf16[128,1024]{1,0:T(8,128)(2,1)S(1)} collective-permute-done((bf16[128,1024]{1,0:T(8,128)(2,1)S(1)}, bf16[128,1024]{1,0:T(8,128)(2,1)S(1)}, u32[]{:S(2)}, u32[]{:S(2)}) %collective-permute-start.19) | collective-permute-done | bytes 262176 | tf_op jit(solution)/shard_map/ppermute | solution.py:87
  153.0 8.8 %collective-permute-done.6 = bf16[128,1024]{1,0:T(8,128)(2,1)S(1)} collective-permute-done((bf16[128,1024]{1,0:T(8,128)(2,1)S(1)}, bf16[128,1024]{1,0:T(8,128)(2,1)S(1)}, u32[]{:S(2)}, u32[]{:S(2)}) %collective-permute-start.6) | collective-permute-done | bytes 262176 | tf_op jit(solution)/shard_map/ppermute | solution.py:87
  162.8 3.4 collective-permute-start.10
  166.2 4.3 collective-permute-done.11
  170.5 6.5 %collective-permute-done.10 = bf16[128,1024]{1,0:T(8,128)(2,1)S(1)} collective-permute-done((bf16[128,1024]{1,0:T(8,128)(2,1)S(1)}, bf16[128,1024]{1,0:T(8,128)(2,1)S(1)}, u32[]{:S(2)}, u32[]{:S(2)}) %collective-permute-start.10) | collective-permute-done | bytes 262176 | tf_op jit(solution)/shard_map/ppermute | solution.py:87
  182.0 4.1 fusion.46
  186.1 3.8 multiply_convert_fusion.1
  189.9 3.7 convolution_convert_fusion.1
  195.2 3.1 convolution_convert_fusion.3
  198.4 2.9 fusion.154
  206.3 3.7 collective-permute-done.22
  210.0 6.0 %collective-permute-done.23 = bf16[128,1024]{1,0:T(8,128)(2,1)S(1)} collective-permute-done((bf16[128,1024]{1,0:T(8,128)(2,1)S(1)}, bf16[128,1024]{1,0:T(8,128)(2,1)S(1)}, u32[]{:S(2)}, u32[]{:S(2)}) %collective-permute-start.23) | collective-permute-done | bytes 262176 | tf_op jit(solution)/shard_map/ppermute | solution.py:87
  221.9 3.1 collective-permute-done.27
  225.0 5.7 %collective-permute-done.26 = bf16[128,1024]{1,0:T(8,128)(2,1)S(1)} collective-permute-done((bf16[128,1024]{1,0:T(8,128)(2,1)S(1)}, bf16[128,1024]{1,0:T(8,128)(2,1)S(1)}, u32[]{:S(2)}, u32[]{:S(2)}) %collective-permute-start.26) | collective-permute-done | bytes 262176 | tf_op jit(solution)/shard_map/ppermute | solution.py:87
  236.4 7.9 %all-to-all-start.5 = ((bf16[128,8,1152]{2,1,0:T(8,128)(2,1)}), bf16[128,8,1152]{2,1,0:T(8,128)(2,1)}, u32[]{:S(2)}, u32[]{:S(2)}) async-start(bf16[128,8,1152]{2,1,0:T(8,128)(2,1)} %pad_maximum_fusion), calls=%async_computation.5 | async-start | bytes 4718592 | tf_op jit(solution)/shard_map/all_to_all | solution.py:116
  244.4 3.8 fusion.156
  256.1 54.1 %while.29 = (s32[]{:T(128)}, f32[2048,128]{1,0:T(8,128)}, f32[2048,128]{1,0:T(8,128)}, f32[2,1024,128]{2,1,0:T(8,128)}, bf16[2,1024,128]{2,1,0:T(8,128)(2,1)S(1)...) while((s32[]{:T(128)}, f32[2048,128]{1,0:T(8,128)}, ...), condition=%wide.region_12.13_spmd.clone, body=%wide.region_10.12_spmd.clone.sunk | while | flops 2706766848 | bytes 120619320 | solution.py:261
  258.5 6.6 %multiply_reduce_fusion.12 = (f32[1024]{0:T(1024)S(1)}, f32[1024,2048]{1,0:T(8,128)}) fusion(f32[1024,2048]{1,0:T(8,128)S(1)} %fusion.206, f32[1024]{0:T(1024)S(1)} %bitcast.256, bf16[2048,128]{1,0:T(8,128)(2,1)} %get-tuple-element.588, bf16[2,1024,128]{2,1,0:T(8,128)(2,1)S(1)} %get-tuple-element.587, s32[]{:T(128)S(6)} %copy.158, ...), kind=kOutput, calls=%fused_computation.18.clone.1 | convolution fusion | flops 549452800 | bytes 17584132 | tf_op jit(solution)/shard_map/while/body/eval_jaxpr/dot_general | solution.py:40
  265.2 6.6 %multiply_convert_fusion.7 = bf16[1024,2048]{1,0:T(8,128)(2,1)S(1)} fusion(f32[1024,2048]{1,0:T(8,128)} %get-tuple-element.525, f32[1024,2048]{1,0:T(8,128)} %copy-done.2, f32[1024]{0:T(1024)S(1)} %get-tuple-element.526), kind=kLoop, calls=%fused_computation.17.clone.1 | loop fusion | flops 6291456 | bytes 20975616 | tf_op jit(solution)/shard_map/while/body/eval_jaxpr/convert_element_type | solution.py:254
  271.7 5.8 %fusion.208 = f32[2048,128]{1,0:T(8,128)} fusion(f32[1024,2048]{1,0:T(8,128)} %get-tuple-element.525, f32[2048,128]{1,0:T(8,128)} %get-tuple-element.572, pred[]{:T(512)S(6)} %compare.3, bf16[2,1024,128]{2,1,0:T(8,128)(2,1)} %get-tuple-element.590, s32[]{:T(128)S(6)} %copy.158), kind=kOutput, calls=%fused_computation.24.clone.1 | convolution fusion | flops 539492352 | bytes 10747909 | tf_op jit(solution)/shard_map/while/body/eval_jaxpr/dot_general | solution.py:40
  285.4 6.6 %multiply_reduce_fusion.12 = (f32[1024]{0:T(1024)S(1)}, f32[1024,2048]{1,0:T(8,128)}) fusion(f32[1024,2048]{1,0:T(8,128)S(1)} %fusion.206, f32[1024]{0:T(1024)S(1)} %bitcast.256, bf16[2048,128]{1,0:T(8,128)(2,1)} %get-tuple-element.588, bf16[2,1024,128]{2,1,0:T(8,128)(2,1)S(1)} %get-tuple-element.587, s32[]{:T(128)S(6)} %copy.158, ...), kind=kOutput, calls=%fused_computation.18.clone.1 | convolution fusion | flops 549452800 | bytes 17584132 | tf_op jit(solution)/shard_map/while/body/eval_jaxpr/dot_general | solution.py:40
  292.1 6.6 %multiply_convert_fusion.7 = bf16[1024,2048]{1,0:T(8,128)(2,1)S(1)} fusion(f32[1024,2048]{1,0:T(8,128)} %get-tuple-element.525, f32[1024,2048]{1,0:T(8,128)} %copy-done.2, f32[1024]{0:T(1024)S(1)} %get-tuple-element.526), kind=kLoop, calls=%fused_computation.17.clone.1 | loop fusion | flops 6291456 | bytes 20975616 | tf_op jit(solution)/shard_map/while/body/eval_jaxpr/convert_element_type | solution.py:254
  298.6 6.1 %fusion.208 = f32[2048,128]{1,0:T(8,128)} fusion(f32[1024,2048]{1,0:T(8,128)} %get-tuple-element.525, f32[2048,128]{1,0:T(8,128)} %get-tuple-element.572, pred[]{:T(512)S(6)} %compare.3, bf16[2,1024,128]{2,1,0:T(8,128)(2,1)} %get-tuple-element.590, s32[]{:T(128)S(6)} %copy.158), kind=kOutput, calls=%fused_computation.24.clone.1 | convolution fusion | flops 539492352 | bytes 10747909 | tf_op jit(solution)/shard_map/while/body/eval_jaxpr/dot_general | solution.py:40
  313.1 3.1 collective-permute-start.29
  330.6 10.8 %all-to-all-start.4 = ((bf16[128,8,256]{2,1,0:T(8,128)(2,1)}), bf16[128,8,256]{2,1,0:T(8,128)(2,1)S(1)}, u32[]{:S(2)}, u32[]{:S(2)}) async-start(bf16[128,8,256]{2,1,0:T(8,128)(2,1)} %fusion.42), calls=%async_computation.4 | async-start | bytes 1048576 | tf_op jit(solution)/shard_map/all_to_all | solution.py:116
  343.4 4.2 fusion.40
  347.6 7.5 %all-to-all-done.4 = bf16[128,8,256]{2,1,0:T(8,128)(2,1)S(1)} async-done(((bf16[128,8,256]{2,1,0:T(8,128)(2,1)}), bf16[128,8,256]{2,1,0:T(8,128)(2,1)S(1)}, u32[]{:S(2)}, u32[]{:S(2)}) %all-to-all-start.4) | async-done | bytes 524320 | tf_op jit(solution)/shard_map/all_to_all | solution.py:116
  355.1 4.5 %all-to-all-start.3 = ((bf16[128,8,512]{2,1,0:T(8,128)(2,1)}), bf16[128,8,512]{2,1,0:T(8,128)(2,1)S(1)}, u32[]{:S(2)}, u32[]{:S(2)}) async-start(bf16[128,8,512]{2,1,0:T(8,128)(2,1)} %fusion.40), calls=%async_computation.3 | async-start | bytes 2097152 | tf_op jit(solution)/shard_map/all_to_all | solution.py:116
  365.9 12.9 %all-to-all-done.3 = bf16[128,8,512]{2,1,0:T(8,128)(2,1)S(1)} async-done(((bf16[128,8,512]{2,1,0:T(8,128)(2,1)}), bf16[128,8,512]{2,1,0:T(8,128)(2,1)S(1)}, u32[]{:S(2)}, u32[]{:S(2)}) %all-to-all-start.3) | async-done | bytes 1048608 | tf_op jit(solution)/shard_map/all_to_all | solution.py:116
  386.7 4.6 %collective-permute-done.31 = bf16[128,1024]{1,0:T(8,128)(2,1)S(1)} collective-permute-done((bf16[128,1024]{1,0:T(8,128)(2,1)S(1)}, bf16[128,1024]{1,0:T(8,128)(2,1)S(1)}, u32[]{:S(2)}, u32[]{:S(2)}) %collective-permute-start.31) | collective-permute-done | bytes 262176 | tf_op jit(solution)/shard_map/ppermute | solution.py:87
  391.3 6.1 %collective-permute-done.32 = bf16[128,1024]{1,0:T(8,128)(2,1)S(1)} collective-permute-done((bf16[128,1024]{1,0:T(8,128)(2,1)S(1)}, bf16[128,1024]{1,0:T(8,128)(2,1)S(1)}, u32[]{:S(2)}, u32[]{:S(2)}) %collective-permute-start.32) | collective-permute-done | bytes 262176 | tf_op jit(solution)/shard_map/ppermute | solution.py:87
  398.4 11.3 %all-to-all-start.6 = ((f32[128,1,18]{2,1,0:T(1,128)}), f32[128,1,18]{2,1,0:T(1,128)S(1)}, u32[]{:S(2)}, u32[]{:S(2)}) async-start(f32[128,1,18]{2,1,0:T(1,128)} %bitcast.64), calls=%async_computation.6 | async-start | bytes 131072 | tf_op jit(solution)/shard_map/all_to_all | solution.py:295
  409.7 9.5 %all-to-all-done.6 = f32[128,1,18]{2,1,0:T(1,128)S(1)} async-done(((f32[128,1,18]{2,1,0:T(1,128)}), f32[128,1,18]{2,1,0:T(1,128)S(1)}, u32[]{:S(2)}, u32[]{:S(2)}) %all-to-all-start.6) | async-done | bytes 9248 | tf_op jit(solution)/shard_map/all_to_all | solution.py:295
  422.0 4.5 %all-to-all-start.7 = ((f32[128,1,128]{2,1,0:T(1,128)}), f32[128,1,128]{2,1,0:T(1,128)S(1)}, u32[]{:S(2)}, u32[]{:S(2)}) async-start(f32[128,1,128]{2,1,0:T(1,128)} %broadcast_in_dim.52), calls=%async_computation.7 | async-start | bytes 131072 | tf_op jit(solution)/shard_map/all_to_all | solution.py:310
  427.2 2.7 fusion.83
  429.9 6.1 %all-to-all-done.7 = f32[128,1,128]{2,1,0:T(1,128)S(1)} async-done(((f32[128,1,128]{2,1,0:T(1,128)}), f32[128,1,128]{2,1,0:T(1,128)S(1)}, u32[]{:S(2)}, u32[]{:S(2)}) %all-to-all-start.7) | async-done | bytes 65568 | tf_op jit(solution)/shard_map/all_to_all | solution.py:310
  (385 shorter events, 142.2 us)
Async XLA Ops:
  0.7 23.4 %collective-permute-start.2 = (bf16[128,1024]{1,0:T(8,128)(2,1)}, bf16[128,1024]{1,0:T(8,128)(2,1)S(1)}, u32[]{:S(2)}, u32[]{:S(2)}) collective-permute-start(bf16[128,1024]{1,0:T(8,128)(2,1)} %bitcast.237), channel_id=1, source_target_pairs={{0,2},{2,4},{4,6},{6,0},{1,3},{3,5},{5,7},{7,1},{8,10},{10,12},{12... | collective-permute-start | bytes 786440 | tf_op jit(solution)/shard_map/ppermute | solution.py:87
  2.8 21.3 %collective-permute-start.1 = (bf16[128,1024]{1,0:T(8,128)(2,1)}, bf16[128,1024]{1,0:T(8,128)(2,1)S(1)}, u32[]{:S(2)}, u32[]{:S(2)}) collective-permute-start(bf16[128,1024]{1,0:T(8,128)(2,1)} %bitcast.238), channel_id=1, source_target_pairs={{0,4},{2,6},{4,0},{6,2},{1,5},{3,7},{5,1},{7,3},{8,12},{10,14},{12... | collective-permute-start | bytes 786440 | tf_op jit(solution)/shard_map/ppermute | solution.py:87
  5.2 18.8 %collective-permute-start = (bf16[128,1024]{1,0:T(8,128)(2,1)}, bf16[128,1024]{1,0:T(8,128)(2,1)S(1)}, u32[]{:S(2)}, u32[]{:S(2)}) collective-permute-start(bf16[128,1024]{1,0:T(8,128)(2,1)} %bitcast.239), channel_id=1, source_target_pairs={{0,6},{2,0},{4,2},{6,4},{1,7},{3,1},{5,3},{7,5},{8,14},{10,8},{12,... | collective-permute-start | bytes 786440 | tf_op jit(solution)/shard_map/ppermute | solution.py:87
  7.7 19.4 %all-to-all-start = ((bf16[128,1,18]{2,1,0:T(2,128)(2,1)}), bf16[128,1,18]{2,1,0:T(2,128)(2,1)S(1)}, u32[]{:S(2)}, u32[]{:S(2)}) async-start(bf16[128,1,18]{2,1,0:T(2,128)(2,1)} %broadcast_in_dim.45), calls=%async_computation | async-start | bytes 131072 | tf_op jit(solution)/shard_map/all_to_all | solution.py:166
  16.8 51.5 %copy-start.78 = (f32[64]{0:T(128)}, f32[64]{0:T(128)S(1)}, u32[]{:S(2)}) copy-start(f32[64]{0:T(128)S(1)} %multiply_exponential_fusion) | copy-start | bytes 772
  20.3 48.0 %copy-start.61 = (f32[1024]{0:T(1024)}, f32[1024]{0:T(1024)S(1)}, u32[]{:S(2)}) copy-start(f32[1024]{0:T(1024)S(1)} %convert_element_type.176) | copy-start | bytes 12292
  24.0 50.3 %copy-start.17 = (f32[1024,64]{1,0:T(8,128)}, f32[1024,64]{1,0:T(8,128)S(1)}, u32[]{:S(2)}) copy-start(f32[1024,64]{1,0:T(8,128)S(1)} %get-tuple-element.392) | copy-start | bytes 786436
  25.2 16.4 %collective-permute-start.3 = (bf16[512,1024]{1,0:T(8,128)(2,1)}, bf16[512,1024]{1,0:T(8,128)(2,1)S(1)}, u32[]{:S(2)}, u32[]{:S(2)}) collective-permute-start(bf16[512,1024]{1,0:T(8,128)(2,1)} %pad_maximum_fusion.6), channel_id=1, source_target_pairs={{0,1},{1,0},{2,3},{3,2},{4,5},{5,4},{6,7},{7,6},{8,9},{9,8},{10,11... | collective-permute-start | bytes 3145736 | tf_op jit(solution)/shard_map/ppermute | solution.py:79
  28.1 28.1 %all-to-all-start.1 = ((bf16[128,8,512]{2,1,0:T(8,128)(2,1)}), bf16[128,8,512]{2,1,0:T(8,128)(2,1)S(1)}, u32[]{:S(2)}, u32[]{:S(2)}) async-start(bf16[128,8,512]{2,1,0:T(8,128)(2,1)} %bitcast.6), calls=%async_computation.1 | async-start | bytes 2097152 | tf_op jit(solution)/shard_map/all_to_all | solution.py:111
  58.1 75.1 %all-to-all-start.2 = ((bf16[128,8,1408]{2,1,0:T(8,128)(2,1)}), bf16[128,8,1408]{2,1,0:T(8,128)(2,1)}, u32[]{:S(2)}, u32[]{:S(2)}) async-start(bf16[128,8,1408]{2,1,0:T(8,128)(2,1)} %bitcast.25), calls=%async_computation.2 | async-start | bytes 5767168 | tf_op jit(solution)/shard_map/all_to_all | solution.py:111
  70.4 40.4 %collective-permute-start.4 = (bf16[1024,256]{0,1:T(8,128)(2,1)}, bf16[1024,256]{0,1:T(8,128)(2,1)}, u32[]{:S(2)}, u32[]{:S(2)}) collective-permute-start(bf16[1024,256]{0,1:T(8,128)(2,1)} %pad_maximum_fusion.13), channel_id=1, source_target_pairs={{0,8},{8,0},{1,9},{9,1},{2,10},{10,2},{3,11},{11,3},{4,12},{12,4},... | collective-permute-start | bytes 1572872 | tf_op jit(solution)/shard_map/ppermute | solution.py:83
  135.0 3.6 collective-permute-start.5
  135.9 14.7 %collective-permute-start.19 = (bf16[128,1024]{1,0:T(8,128)(2,1)S(1)}, bf16[128,1024]{1,0:T(8,128)(2,1)S(1)}, u32[]{:S(2)}, u32[]{:S(2)}) collective-permute-start(bf16[128,1024]{1,0:T(8,128)(2,1)S(1)} %bitcast.243), channel_id=1, source_target_pairs={{0,2},{2,4},{4,6},{6,0},{1,3},{3,5},{5,7},{7,1},{8,10},{10,12},{12... | collective-permute-start | bytes 786440 | tf_op jit(solution)/shard_map/ppermute | solution.py:87
  135.9 14.7 %collective-permute-start.18 = (bf16[128,1024]{1,0:T(8,128)(2,1)S(1)}, bf16[128,1024]{1,0:T(8,128)(2,1)S(1)}, u32[]{:S(2)}, u32[]{:S(2)}) collective-permute-start(bf16[128,1024]{1,0:T(8,128)(2,1)S(1)} %bitcast.244), channel_id=1, source_target_pairs={{0,4},{2,6},{4,0},{6,2},{1,5},{3,7},{5,1},{7,3},{8,12},{10,14},{12... | collective-permute-start | bytes 786440 | tf_op jit(solution)/shard_map/ppermute | solution.py:87
  137.3 13.6 %collective-permute-start.17 = (bf16[128,1024]{1,0:T(8,128)(2,1)S(1)}, bf16[128,1024]{1,0:T(8,128)(2,1)S(1)}, u32[]{:S(2)}, u32[]{:S(2)}) collective-permute-start(bf16[128,1024]{1,0:T(8,128)(2,1)S(1)} %bitcast.245), channel_id=1, source_target_pairs={{0,6},{2,0},{4,2},{6,4},{1,7},{3,1},{5,3},{7,5},{8,14},{10,8},{12,... | collective-permute-start | bytes 786440 | tf_op jit(solution)/shard_map/ppermute | solution.py:87
  140.2 21.6 %collective-permute-start.6 = (bf16[128,1024]{1,0:T(8,128)(2,1)S(1)}, bf16[128,1024]{1,0:T(8,128)(2,1)S(1)}, u32[]{:S(2)}, u32[]{:S(2)}) collective-permute-start(bf16[128,1024]{1,0:T(8,128)(2,1)S(1)} %get-tuple-element.362), channel_id=1, source_target_pairs={{0,2},{2,4},{4,6},{6,0},{1,3},{3,5},{5,7},{7,1},{8,10},{10,12},{12... | collective-permute-start | bytes 786440 | tf_op jit(solution)/shard_map/ppermute | solution.py:87
  140.9 21.0 %collective-permute-start.8 = (bf16[128,1024]{1,0:T(8,128)(2,1)S(1)}, bf16[128,1024]{1,0:T(8,128)(2,1)S(1)}, u32[]{:S(2)}, u32[]{:S(2)}) collective-permute-start(bf16[128,1024]{1,0:T(8,128)(2,1)S(1)} %get-tuple-element.363), channel_id=1, source_target_pairs={{0,6},{2,0},{4,2},{6,4},{1,7},{3,1},{5,3},{7,5},{8,14},{10,8},{12,... | collective-permute-start | bytes 786440 | tf_op jit(solution)/shard_map/ppermute | solution.py:87
  150.6 11.2 %collective-permute-start.7 = (bf16[128,1024]{1,0:T(8,128)(2,1)S(1)}, bf16[128,1024]{1,0:T(8,128)(2,1)S(1)}, u32[]{:S(2)}, u32[]{:S(2)}) collective-permute-start(bf16[128,1024]{1,0:T(8,128)(2,1)S(1)} %get-tuple-element.364), channel_id=1, source_target_pairs={{0,4},{2,6},{4,0},{6,2},{1,5},{3,7},{5,1},{7,3},{8,12},{10,14},{12... | collective-permute-start | bytes 786440 | tf_op jit(solution)/shard_map/ppermute | solution.py:87
  151.0 28.8 %collective-permute-start.20 = (bf16[512,1024]{1,0:T(8,128)(2,1)S(1)}, bf16[512,1024]{1,0:T(8,128)(2,1)S(1)}, u32[]{:S(2)}, u32[]{:S(2)}) collective-permute-start(bf16[512,1024]{1,0:T(8,128)(2,1)S(1)} %pad_maximum_fusion.9), channel_id=1, source_target_pairs={{0,1},{1,0},{2,3},{3,2},{4,5},{5,4},{6,7},{7,6},{8,9},{9,8},{10,11... | collective-permute-start | bytes 3145736 | tf_op jit(solution)/shard_map/ppermute | solution.py:79
  162.1 54.2 %copy-start.8 = (f32[128,1024]{1,0:T(8,128)}, f32[128,1024]{1,0:T(8,128)S(1)}, u32[]{:S(2)}) copy-start(f32[128,1024]{1,0:T(8,128)S(1)} %get-tuple-element.339) | copy-start | bytes 1572868
  162.3 8.2 %collective-permute-start.11 = (bf16[128,1024]{1,0:T(8,128)(2,1)S(1)}, bf16[128,1024]{1,0:T(8,128)(2,1)S(1)}, u32[]{:S(2)}, u32[]{:S(2)}) collective-permute-start(bf16[128,1024]{1,0:T(8,128)(2,1)S(1)} %get-tuple-element.337), channel_id=1, source_target_pairs={{0,2},{2,4},{4,6},{6,0},{1,3},{3,5},{5,7},{7,1},{8,10},{10,12},{12... | collective-permute-start | bytes 786440 | tf_op jit(solution)/shard_map/ppermute | solution.py:87
  162.8 14.2 %collective-permute-start.10 = (bf16[128,1024]{1,0:T(8,128)(2,1)S(1)}, bf16[128,1024]{1,0:T(8,128)(2,1)S(1)}, u32[]{:S(2)}, u32[]{:S(2)}) collective-permute-start(bf16[128,1024]{1,0:T(8,128)(2,1)S(1)} %get-tuple-element.337), channel_id=1, source_target_pairs={{0,4},{2,6},{4,0},{6,2},{1,5},{3,7},{5,1},{7,3},{8,12},{10,14},{12... | collective-permute-start | bytes 786440 | tf_op jit(solution)/shard_map/ppermute | solution.py:87
  166.2 10.8 %collective-permute-start.9 = (bf16[128,1024]{1,0:T(8,128)(2,1)S(1)}, bf16[128,1024]{1,0:T(8,128)(2,1)S(1)}, u32[]{:S(2)}, u32[]{:S(2)}) collective-permute-start(bf16[128,1024]{1,0:T(8,128)(2,1)S(1)} %get-tuple-element.337), channel_id=1, source_target_pairs={{0,6},{2,0},{4,2},{6,4},{1,7},{3,1},{5,3},{7,5},{8,14},{10,8},{12,... | collective-permute-start | bytes 786440 | tf_op jit(solution)/shard_map/ppermute | solution.py:87
  177.2 4.8 %collective-permute-start.12 = (bf16[512,1024]{1,0:T(8,128)(2,1)S(1)}, bf16[512,1024]{1,0:T(8,128)(2,1)S(1)}, u32[]{:S(2)}, u32[]{:S(2)}) collective-permute-start(bf16[512,1024]{1,0:T(8,128)(2,1)S(1)} %pad_maximum_fusion.8), channel_id=1, source_target_pairs={{0,1},{1,0},{2,3},{3,2},{4,5},{5,4},{6,7},{7,6},{8,9},{9,8},{10,11... | collective-permute-start | bytes 3145736 | tf_op jit(solution)/shard_map/ppermute | solution.py:79
  193.6 4.7 %collective-permute-start.21 = (bf16[512,1024]{1,0:T(8,128)(2,1)}, bf16[512,1024]{1,0:T(8,128)(2,1)}, u32[]{:S(2)}, u32[]{:S(2)}) collective-permute-start(bf16[512,1024]{1,0:T(8,128)(2,1)} %convolution_convert_fusion.1), channel_id=1, source_target_pairs={{0,1},{1,0},{2,3},{3,2},{4,5},{5,4},{6,7},{7,6},{8,9},{9,8},{10,11... | collective-permute-start | bytes 3145736 | tf_op jit(solution)/shard_map/ppermute | solution.py:79
  198.2 46.1 %collective-permute-start.13 = (bf16[512,1024]{1,0:T(8,128)(2,1)}, bf16[512,1024]{1,0:T(8,128)(2,1)}, u32[]{:S(2)}, u32[]{:S(2)}) collective-permute-start(bf16[512,1024]{1,0:T(8,128)(2,1)} %convolution_convert_fusion.3), channel_id=1, source_target_pairs={{0,1},{1,0},{2,3},{3,2},{4,5},{5,4},{6,7},{7,6},{8,9},{9,8},{10,11... | collective-permute-start | bytes 3145736 | tf_op jit(solution)/shard_map/ppermute | solution.py:79
  201.3 8.7 %collective-permute-start.22 = (bf16[128,1024]{1,0:T(8,128)(2,1)S(1)}, bf16[128,1024]{1,0:T(8,128)(2,1)S(1)}, u32[]{:S(2)}, u32[]{:S(2)}) collective-permute-start(bf16[128,1024]{1,0:T(8,128)(2,1)S(1)} %get-tuple-element.356), channel_id=1, source_target_pairs={{0,2},{2,4},{4,6},{6,0},{1,3},{3,5},{5,7},{7,1},{8,10},{10,12},{12... | collective-permute-start | bytes 786440 | tf_op jit(solution)/shard_map/ppermute | solution.py:87
  201.4 8.6 %collective-permute-start.24 = (bf16[128,1024]{1,0:T(8,128)(2,1)S(1)}, bf16[128,1024]{1,0:T(8,128)(2,1)S(1)}, u32[]{:S(2)}, u32[]{:S(2)}) collective-permute-start(bf16[128,1024]{1,0:T(8,128)(2,1)S(1)} %get-tuple-element.357), channel_id=1, source_target_pairs={{0,6},{2,0},{4,2},{6,4},{1,7},{3,1},{5,3},{7,5},{8,14},{10,8},{12,... | collective-permute-start | bytes 786440 | tf_op jit(solution)/shard_map/ppermute | solution.py:87
  204.0 12.0 %collective-permute-start.23 = (bf16[128,1024]{1,0:T(8,128)(2,1)S(1)}, bf16[128,1024]{1,0:T(8,128)(2,1)S(1)}, u32[]{:S(2)}, u32[]{:S(2)}) collective-permute-start(bf16[128,1024]{1,0:T(8,128)(2,1)S(1)} %get-tuple-element.358), channel_id=1, source_target_pairs={{0,4},{2,6},{4,0},{6,2},{1,5},{3,7},{5,1},{7,3},{8,12},{10,14},{12... | collective-permute-start | bytes 786440 | tf_op jit(solution)/shard_map/ppermute | solution.py:87
  217.3 7.7 %collective-permute-start.27 = (bf16[128,1024]{1,0:T(8,128)(2,1)S(1)}, bf16[128,1024]{1,0:T(8,128)(2,1)S(1)}, u32[]{:S(2)}, u32[]{:S(2)}) collective-permute-start(bf16[128,1024]{1,0:T(8,128)(2,1)S(1)} %get-tuple-element.334), channel_id=1, source_target_pairs={{0,2},{2,4},{4,6},{6,0},{1,3},{3,5},{5,7},{7,1},{8,10},{10,12},{12... | collective-permute-start | bytes 786440 | tf_op jit(solution)/shard_map/ppermute | solution.py:87
  217.8 12.9 %collective-permute-start.26 = (bf16[128,1024]{1,0:T(8,128)(2,1)S(1)}, bf16[128,1024]{1,0:T(8,128)(2,1)S(1)}, u32[]{:S(2)}, u32[]{:S(2)}) collective-permute-start(bf16[128,1024]{1,0:T(8,128)(2,1)S(1)} %get-tuple-element.334), channel_id=1, source_target_pairs={{0,4},{2,6},{4,0},{6,2},{1,5},{3,7},{5,1},{7,3},{8,12},{10,14},{12... | collective-permute-start | bytes 786440 | tf_op jit(solution)/shard_map/ppermute | solution.py:87
  220.4 11.5 %collective-permute-start.25 = (bf16[128,1024]{1,0:T(8,128)(2,1)S(1)}, bf16[128,1024]{1,0:T(8,128)(2,1)S(1)}, u32[]{:S(2)}, u32[]{:S(2)}) collective-permute-start(bf16[128,1024]{1,0:T(8,128)(2,1)S(1)} %get-tuple-element.334), channel_id=1, source_target_pairs={{0,6},{2,0},{4,2},{6,4},{1,7},{3,1},{5,3},{7,5},{8,14},{10,8},{12,... | collective-permute-start | bytes 786440 | tf_op jit(solution)/shard_map/ppermute | solution.py:87
  232.7 19.2 %collective-permute-start.28 = (bf16[512,1024]{1,0:T(8,128)(2,1)S(1)}, bf16[512,1024]{1,0:T(8,128)(2,1)S(1)}, u32[]{:S(2)}, u32[]{:S(2)}) collective-permute-start(bf16[512,1024]{1,0:T(8,128)(2,1)S(1)} %pad_maximum_fusion.10), channel_id=1, source_target_pairs={{0,1},{1,0},{2,3},{3,2},{4,5},{5,4},{6,7},{7,6},{8,9},{9,8},{10,11... | collective-permute-start | bytes 3145736 | tf_op jit(solution)/shard_map/ppermute | solution.py:79
  236.4 94.1 %all-to-all-start.5 = ((bf16[128,8,1152]{2,1,0:T(8,128)(2,1)}), bf16[128,8,1152]{2,1,0:T(8,128)(2,1)}, u32[]{:S(2)}, u32[]{:S(2)}) async-start(bf16[128,8,1152]{2,1,0:T(8,128)(2,1)} %pad_maximum_fusion), calls=%async_computation.5 | async-start | bytes 4718592 | tf_op jit(solution)/shard_map/all_to_all | solution.py:116
  249.1 177.3 %collective-permute-start.14 = (bf16[128,1024]{1,0:T(8,128)(2,1)}, bf16[128,1024]{1,0:T(8,128)(2,1)}, u32[]{:S(2)}, u32[]{:S(2)}) collective-permute-start(bf16[128,1024]{1,0:T(8,128)(2,1)} %get-tuple-element.359), channel_id=1, source_target_pairs={{0,2},{2,4},{4,6},{6,0},{1,3},{3,5},{5,7},{7,1},{8,10},{10,12},{12... | collective-permute-start | bytes 786440 | tf_op jit(solution)/shard_map/ppermute | solution.py:87
  250.5 175.9 %collective-permute-start.16 = (bf16[128,1024]{1,0:T(8,128)(2,1)}, bf16[128,1024]{1,0:T(8,128)(2,1)}, u32[]{:S(2)}, u32[]{:S(2)}) collective-permute-start(bf16[128,1024]{1,0:T(8,128)(2,1)} %get-tuple-element.360), channel_id=1, source_target_pairs={{0,6},{2,0},{4,2},{6,4},{1,7},{3,1},{5,3},{7,5},{8,14},{10,8},{12,... | collective-permute-start | bytes 786440 | tf_op jit(solution)/shard_map/ppermute | solution.py:87
  313.1 13.7 %collective-permute-start.29 = (bf16[1024,256]{0,1:T(8,128)(2,1)}, bf16[1024,256]{0,1:T(8,128)(2,1)}, u32[]{:S(2)}, u32[]{:S(2)}) collective-permute-start(bf16[1024,256]{0,1:T(8,128)(2,1)} %fusion.56), channel_id=1, source_target_pairs={{0,8},{8,0},{1,9},{9,1},{2,10},{10,2},{3,11},{11,3},{4,12},{12,4},... | collective-permute-start | bytes 1572872 | tf_op jit(solution)/shard_map/ppermute | solution.py:83
  330.6 24.5 %all-to-all-start.4 = ((bf16[128,8,256]{2,1,0:T(8,128)(2,1)}), bf16[128,8,256]{2,1,0:T(8,128)(2,1)S(1)}, u32[]{:S(2)}, u32[]{:S(2)}) async-start(bf16[128,8,256]{2,1,0:T(8,128)(2,1)} %fusion.42), calls=%async_computation.4 | async-start | bytes 1048576 | tf_op jit(solution)/shard_map/all_to_all | solution.py:116
  355.1 23.8 %all-to-all-start.3 = ((bf16[128,8,512]{2,1,0:T(8,128)(2,1)}), bf16[128,8,512]{2,1,0:T(8,128)(2,1)S(1)}, u32[]{:S(2)}, u32[]{:S(2)}) async-start(bf16[128,8,512]{2,1,0:T(8,128)(2,1)} %fusion.40), calls=%async_computation.3 | async-start | bytes 2097152 | tf_op jit(solution)/shard_map/all_to_all | solution.py:116
  364.8 16.1 %collective-permute-start.30 = (bf16[512,1024]{1,0:T(8,128)(2,1)}, bf16[512,1024]{1,0:T(8,128)(2,1)}, u32[]{:S(2)}, u32[]{:S(2)}) collective-permute-start(bf16[512,1024]{1,0:T(8,128)(2,1)} %convolution_convert_fusion.5), channel_id=1, source_target_pairs={{0,1},{1,0},{2,3},{3,2},{4,5},{5,4},{6,7},{7,6},{8,9},{9,8},{10,11... | collective-permute-start | bytes 3145736 | tf_op jit(solution)/shard_map/ppermute | solution.py:79
  383.1 44.1 %copy-start.9 = (f32[128,1024]{1,0:T(8,128)S(1)}, f32[128,1024]{1,0:T(8,128)}, u32[]{:S(2)}) copy-start(f32[128,1024]{1,0:T(8,128)} %copy-done.8) | copy-start | bytes 1572868
  383.1 44.1 %copy-start.20 = (f32[128,1024]{1,0:T(8,128)S(1)}, f32[128,1024]{1,0:T(8,128)}, u32[]{:S(2)}) copy-start(f32[128,1024]{1,0:T(8,128)} %copy-done.19) | copy-start | bytes 1572868
  383.2 8.1 %collective-permute-start.31 = (bf16[128,1024]{1,0:T(8,128)(2,1)S(1)}, bf16[128,1024]{1,0:T(8,128)(2,1)S(1)}, u32[]{:S(2)}, u32[]{:S(2)}) collective-permute-start(bf16[128,1024]{1,0:T(8,128)(2,1)S(1)} %get-tuple-element.353), channel_id=1, source_target_pairs={{0,2},{2,4},{4,6},{6,0},{1,3},{3,5},{5,7},{7,1},{8,10},{10,12},{12... | collective-permute-start | bytes 786440 | tf_op jit(solution)/shard_map/ppermute | solution.py:87
  383.4 7.9 %collective-permute-start.33 = (bf16[128,1024]{1,0:T(8,128)(2,1)S(1)}, bf16[128,1024]{1,0:T(8,128)(2,1)S(1)}, u32[]{:S(2)}, u32[]{:S(2)}) collective-permute-start(bf16[128,1024]{1,0:T(8,128)(2,1)S(1)} %get-tuple-element.354), channel_id=1, source_target_pairs={{0,6},{2,0},{4,2},{6,4},{1,7},{3,1},{5,3},{7,5},{8,14},{10,8},{12,... | collective-permute-start | bytes 786440 | tf_op jit(solution)/shard_map/ppermute | solution.py:87
  385.9 11.4 %collective-permute-start.32 = (bf16[128,1024]{1,0:T(8,128)(2,1)S(1)}, bf16[128,1024]{1,0:T(8,128)(2,1)S(1)}, u32[]{:S(2)}, u32[]{:S(2)}) collective-permute-start(bf16[128,1024]{1,0:T(8,128)(2,1)S(1)} %get-tuple-element.355), channel_id=1, source_target_pairs={{0,4},{2,6},{4,0},{6,2},{1,5},{3,7},{5,1},{7,3},{8,12},{10,14},{12... | collective-permute-start | bytes 786440 | tf_op jit(solution)/shard_map/ppermute | solution.py:87
  391.3 35.2 %collective-permute-start.15 = (bf16[128,1024]{1,0:T(8,128)(2,1)}, bf16[128,1024]{1,0:T(8,128)(2,1)S(1)}, u32[]{:S(2)}, u32[]{:S(2)}) collective-permute-start(bf16[128,1024]{1,0:T(8,128)(2,1)} %get-tuple-element.361), channel_id=1, source_target_pairs={{0,4},{2,6},{4,0},{6,2},{1,5},{3,7},{5,1},{7,3},{8,12},{10,14},{12... | collective-permute-start | bytes 786440 | tf_op jit(solution)/shard_map/ppermute | solution.py:87
  398.4 20.8 %all-to-all-start.6 = ((f32[128,1,18]{2,1,0:T(1,128)}), f32[128,1,18]{2,1,0:T(1,128)S(1)}, u32[]{:S(2)}, u32[]{:S(2)}) async-start(f32[128,1,18]{2,1,0:T(1,128)} %bitcast.64), calls=%async_computation.6 | async-start | bytes 131072 | tf_op jit(solution)/shard_map/all_to_all | solution.py:295
  422.0 14.1 %all-to-all-start.7 = ((f32[128,1,128]{2,1,0:T(1,128)}), f32[128,1,128]{2,1,0:T(1,128)S(1)}, u32[]{:S(2)}, u32[]{:S(2)}) async-start(f32[128,1,128]{2,1,0:T(1,128)} %broadcast_in_dim.52), calls=%async_computation.7 | async-start | bytes 131072 | tf_op jit(solution)/shard_map/all_to_all | solution.py:310
  (85 other events, 643.5 us)

commit v2 on v1

v2 whole, which is shorter than its diff:
```python
import functools
import math

import jax
import jax.numpy as jnp
from jax import lax
from jax.experimental import pallas as pl
from jax.experimental.pallas import tpu as pltpu
from jax.sharding import Mesh
from jax.sharding import PartitionSpec as P

D = 1024
FF = 3072
QUERY_HEADS = 16
KEY_VALUE_HEADS = 8
HEAD_SIZE = 128
ADAM_STEP = 10
QKVC = 4096
TP = 8
QW = 256
KW = 128
FW = FF // TP
BLK = 64
TILE = 256

ALL = ("ylo", "z", "yhi", "x", "core")
PLANE = ("ylo", "z", "yhi")
GROUP = ("x", "core")

eps_norm = 1e-06
rope_base = 1000000.0
clip_limit = 1.0
beta_one = 0.9
beta_two = 0.95
adam_eps = 1e-08
decay_rate = 0.1
rate_matrix = 0.06
rate_output = 2.0
rate_gain = 1.0
contract_rows = (((0,), (0,)), ((), ()))
contract_cols = (((1,), (1,)), ((), ()))
f32 = jnp.float32
bf16 = jnp.bfloat16


def dot(a, b, dims=(((1,), (0,)), ((), ()))):
    return lax.dot_general(a, b, dims, preferred_element_type=f32)


def rms_scale(value_rows):
    return lax.rsqrt(jnp.mean(value_rows * value_rows, axis=-1, keepdims=True) + eps_norm)


def norm_back(value_rows, scale, gain, grad_out):
    gain_grad = jnp.sum(grad_out * value_rows * scale, axis=tuple(range(value_rows.ndim - 1)))
    weighted = grad_out * gain
    grad_in = scale * weighted - value_rows * scale * scale * scale * jnp.mean(
        weighted * value_rows, axis=-1, keepdims=True
    )
    return (grad_in, gain_grad)


def turn_tables(blocks):
    half = HEAD_SIZE // 2
    inverse = jnp.exp(jnp.arange(half, dtype=f32) * (-2.0 / HEAD_SIZE) * math.log(rope_base))
    inverse = jnp.concatenate([inverse, inverse])
    coarse = (blocks * BLK).astype(f32)[:, None] * inverse[None, :]
    fine = jnp.arange(BLK, dtype=f32)[:, None] * inverse[None, :]
    sign = jnp.where(jnp.arange(HEAD_SIZE) < half, -1.0, 1.0)
    cos_a, sin_a, cos_b, sin_b = lax.optimization_barrier(
        (jnp.cos(coarse), jnp.sin(coarse), jnp.cos(fine), jnp.sin(fine))
    )
    cos_a, sin_a = cos_a[:, None, :], sin_a[:, None, :]
    cosine = cos_a * cos_b - sin_a * sin_b
    sine = (sin_a * cos_b + cos_a * sin_b) * sign
    return (cosine.reshape(-1, HEAD_SIZE), sine.reshape(-1, HEAD_SIZE))


def swap_core(v):
    return lax.ppermute(v, "core", [(0, 1), (1, 0)])


def swap_yhi(v):
    return lax.ppermute(v, "yhi", [(0, 1), (1, 0)])


def shift_x(v, k):
    return lax.ppermute(v, "x", [(i, (i + k) % 4) for i in range(4)])


def y_index(p):
    return (p % 2) * 2 + p // 2


def shift_y(v, k):
    return lax.ppermute(v, ("ylo", "yhi"), [(y_index(i), y_index((i + k) % 4)) for i in range(4)])


def shift_z(v, k):
    return lax.ppermute(v, "z", [(i, (i + k) % 4) for i in range(4)])


def idle_kernel(*refs):
    pass


def after(v, *waits):
    return pl.pallas_call(
        idle_kernel,
        out_shape=jax.ShapeDtypeStruct(v.shape, v.dtype),
        in_specs=[pl.BlockSpec(memory_space=pl.ANY)] * (1 + len(waits)),
        out_specs=pl.BlockSpec(memory_space=pl.ANY),
        input_output_aliases={0: 0},
        cost_estimate=pl.CostEstimate(flops=0, bytes_accessed=0, transcendentals=0),
        name="after",
    )(v, *waits)


def near_gather(v):
    return jnp.concatenate([v, shift_x(v, -1), shift_x(v, -2), shift_x(v, -3)], axis=0)


def group_gather(v):
    near = near_gather(v)
    return jnp.concatenate([near, swap_core(near)], axis=0)


def group_scatter(left, right, dims):
    half = left.shape[0] // 2
    away = dot(left[half:], right, dims).astype(bf16)
    return group_fold(dot(left[:half], right, dims), away)


def group_fold(near, away):
    piece = near.shape[0] // 4
    near = near + swap_core(away).astype(f32)
    low = near.astype(bf16)
    total = near[:piece]
    for k in (1, 2, 3):
        total = total + shift_x(low[k * piece : (k + 1) * piece], k).astype(f32)
    return total


def to_owners(columns):
    return jnp.transpose(columns, (1, 0, 2)).reshape(64, columns.shape[2])


def to_all(columns):
    n = columns.shape[2]
    return jnp.broadcast_to(to_owners(columns)[None], (16, 64, n)).reshape(1024, n)


def plane_sum(grad):
    n = grad.shape[1]
    got = lax.all_to_all(grad.astype(bf16), PLANE, 0, 0, tiled=True)
    return jnp.sum(got.reshape(16, 64, n).astype(f32), axis=0)


def adam(weight, grad, moment, second, rate, decay):
    moment_new = beta_one * moment + (1.0 - beta_one) * grad
    second_new = beta_two * second + (1.0 - beta_two) * grad * grad
    scaled_m = moment_new / (1.0 - beta_one**ADAM_STEP)
    scaled_v = second_new / (1.0 - beta_two**ADAM_STEP)
    weight_new = weight * (1.0 - rate * decay) - rate * scaled_m / (jnp.sqrt(scaled_v) + adam_eps)
    return (weight_new, moment_new, second_new)


def sort_blocks(table, pair, keys, values):
    for i in range(32):
        spot = pl.ds(pl.multiple_of(table[i] * BLK, BLK), BLK)
        keys[spot, :] = pair[i * BLK : (i + 1) * BLK, :HEAD_SIZE]
        values[spot, :] = pair[i * BLK : (i + 1) * BLK, HEAD_SIZE:]


def flip(v):
    return jnp.transpose(v.astype(f32)).astype(bf16)


def stack_heads(ref, rows):
    return jnp.concatenate([ref[rows, :HEAD_SIZE], ref[rows, HEAD_SIZE:]], axis=0)


def seen(place, first, count):
    key_place = first + lax.broadcasted_iota(jnp.int32, (count, 2 * BLK), 0)
    lane = lax.broadcasted_iota(jnp.int32, (count, 2 * BLK), 1)
    return key_place <= place * BLK + lax.rem(lane, BLK)


def attend_kernel(table, query, pair, out, logsum, keys, values, values_t):
    scale = HEAD_SIZE ** (-0.5)
    sort_blocks(table, pair, keys, values)
    for t in range(8):
        values_t[:, t * TILE : (t + 1) * TILE] = flip(values[t * TILE : (t + 1) * TILE, :])

    def block(i, carry):
        place = table[i]
        rows = pl.ds(pl.multiple_of(i * BLK, BLK), BLK)

        def run(count):
            full = count - TILE
            stacked = stack_heads(query, rows)
            tail = dot(keys[full:count, :], stacked, contract_cols)
            tail = jnp.where(seen(place, full, TILE), tail, -1e30)
            top = jnp.max(tail, axis=0, keepdims=True)
            if full:
                head = dot(keys[:full, :], stacked, contract_cols)
                top = jnp.maximum(top, jnp.max(head, axis=0, keepdims=True))
            tail = jnp.exp((tail - top) * scale)
            total = jnp.sum(tail, axis=0, keepdims=True)
            mixed = dot(values_t[:, full:count], tail.astype(bf16))
            if full:
                head = jnp.exp((head - top) * scale)
                total = total + jnp.sum(head, axis=0, keepdims=True)
                mixed = mixed + dot(values_t[:, :full], head.astype(bf16))
            mixed = jnp.transpose(mixed / total).astype(bf16)
            out[rows, :HEAD_SIZE] = mixed[:BLK]
            out[rows, HEAD_SIZE:] = mixed[BLK:]
            logsum[pl.ds(i, 1), :] = top * scale + jnp.log(total)

        for step in range(8):
            pl.when(lax.div(place, 4) == step)(functools.partial(run, (step + 1) * TILE))
        return carry

    lax.fori_loop(0, 16, block, 0)


def turn(v):
    return jnp.concatenate([v[:, HEAD_SIZE // 2 :], v[:, : HEAD_SIZE // 2]], axis=1)


def head_back(raw, grad, gain, cosine, sine):
    grad = grad * cosine - turn(grad) * sine
    scale = lax.rsqrt(jnp.mean(raw * raw, axis=-1, keepdims=True) + eps_norm)
    gain_grad = jnp.sum(grad * raw * scale, axis=0, keepdims=True)
    weighted = grad * gain
    mean = jnp.mean(weighted * raw, axis=-1, keepdims=True)
    return (scale * weighted - raw * (scale * scale * scale * mean), gain_grad)


def attend_back_kernel(
    table, query, pair, out, logsum,
    query_raw, key_raw, cosine, sine, gains, gain_mlp, plain, mid_near, mid_far, weight_out, idle,
    last, grad_query, grad_own, grad_away,
    keys, values, keys_t, acc_key, acc_value, pair_near, pair_far, query_acc, grad,
):
    scale = HEAD_SIZE ** (-0.5)
    grad[:512, :] = dot(mid_near[...], weight_out[...]).astype(bf16)
    grad[512:, :] = dot(mid_far[...], weight_out[...]).astype(bf16)
    sort_blocks(table, pair, keys, values)
    acc_key[...] = jnp.zeros_like(acc_key)
    acc_value[...] = jnp.zeros_like(acc_value)
    for t in range(8):
        keys_t[:, t * TILE : (t + 1) * TILE] = flip(keys[t * TILE : (t + 1) * TILE, :])

    def block(i, carry):
        place = table[i]
        rows = pl.ds(pl.multiple_of(i * BLK, BLK), BLK)

        def run(count):
            stacked = stack_heads(query, rows)
            back = stack_heads(grad, rows)
            made = stack_heads(out, rows)
            inner = jnp.sum(
                jnp.transpose(back.astype(f32) * made.astype(f32)), axis=0, keepdims=True
            )
            level = logsum[pl.ds(i, 1), :]
            total = jnp.zeros((HEAD_SIZE, 2 * BLK), f32)
            for first in range(0, count, TILE):
                span = slice(first, first + TILE)
                probs = jnp.exp(dot(keys[span, :], stacked, contract_cols) * scale - level)
                if first + TILE == count:
                    probs = jnp.where(seen(place, first, TILE), probs, 0.0)
                grad_p = dot(values[span, :], back, contract_cols)
                grad_s = (probs * (grad_p - inner)).astype(bf16)
                acc_key[span, :] += dot(grad_s, stacked)
                acc_value[span, :] += dot(probs.astype(bf16), back)
                total = total + dot(keys_t[:, span], grad_s)
            total = jnp.transpose(total) * scale
            query_acc[rows, :HEAD_SIZE] = total[:BLK]
            query_acc[rows, HEAD_SIZE:] = total[BLK:]

        for step in range(8):
            pl.when(lax.div(place, 4) == step)(functools.partial(run, (step + 1) * TILE))
        return carry

    lax.fori_loop(0, 16, block, 0)
    for i in range(16):
        rows = slice(i * BLK, (i + 1) * BLK)
        near = pl.ds(pl.multiple_of(table[i] * BLK, BLK), BLK)
        grad_own[rows, :HEAD_SIZE] = acc_key[near, :] * scale
        grad_own[rows, HEAD_SIZE:] = acc_value[near, :]
        far = pl.ds(pl.multiple_of(table[16 + i] * BLK, BLK), BLK)
        pair_far[rows, :HEAD_SIZE] = acc_key[far, :] * scale
        pair_far[rows, HEAD_SIZE:] = acc_value[far, :]
    grad_away[...] = pair_far[...].astype(bf16)

    gain_q = gains[0:1, :]
    gain_k = gains[1:2, :]
    sum_q = jnp.zeros((1, HEAD_SIZE), f32)
    sum_k = jnp.zeros((1, HEAD_SIZE), f32)
    for t in range(4):
        rows = slice(t * TILE, (t + 1) * TILE)
        rows_far = slice(1024 + t * TILE, 1024 + (t + 1) * TILE)
        for h in range(2):
            cols = slice(h * HEAD_SIZE, (h + 1) * HEAD_SIZE)
            made, part = head_back(
                query_raw[rows, cols], query_acc[rows, cols], gain_q, cosine[rows, :], sine[rows, :]
            )
            grad_query[rows, cols] = made.astype(bf16)
            sum_q = sum_q + part
        made, part = head_back(
            key_raw[rows, :], grad_own[rows, :HEAD_SIZE], gain_k, cosine[rows, :], sine[rows, :]
        )
        pair_near[rows, :HEAD_SIZE] = made
        pair_near[rows, HEAD_SIZE:] = grad_own[rows, HEAD_SIZE:]
        sum_k = sum_k + part
        made, part = head_back(
            key_raw[rows_far, :], pair_far[rows, :HEAD_SIZE], gain_k,
            cosine[rows_far, :], sine[rows_far, :],
        )
        pair_far[rows, :HEAD_SIZE] = made
        sum_k = sum_k + part

    def down(ref):
        return jnp.transpose(ref[...].astype(f32)).astype(bf16)

    query_t = down(grad_query)
    near_t = down(pair_near)
    far_t = down(pair_far)
    out_t = down(out)
    for t in range(4):
        rows = slice(t * TILE, (t + 1) * TILE)
        made = dot(query_t, plain[:1024, rows])
        last[rows, :QW] = jnp.transpose(made).astype(bf16)
        made = dot(near_t, plain[:1024, rows]) + dot(far_t, plain[1024:, rows])
        last[rows, QW : 2 * QW] = jnp.transpose(made).astype(bf16)
        made = dot(out_t[:, :512], mid_near[:, rows]) + dot(out_t[:, 512:], mid_far[:, rows])
        last[rows, 2 * QW : 3 * QW] = jnp.transpose(made).astype(bf16)
    last[:, 3 * QW :] = jnp.zeros((1024, 128), bf16)
    lines = [gain_mlp[k : k + 1, :] for k in range(8)] + [sum_q, sum_k]
    row = lax.broadcasted_iota(jnp.int32, (16, HEAD_SIZE), 0)
    for k in range(5):
        made = jnp.zeros((16, HEAD_SIZE), f32)
        for at, line in ((0, lines[2 * k]), (8, lines[2 * k + 1])):
            high = line.astype(bf16).astype(f32)
            made = jnp.where(row == at, high, made)
            made = jnp.where(row == at + 1, line - high, made)
        last[16 * k : 16 * k + 16, 3 * QW :] = made.astype(bf16)


def in_vmem():
    return pl.BlockSpec(memory_space=pltpu.VMEM)


def in_smem():
    return pl.BlockSpec(memory_space=pltpu.SMEM)


def project_kernel(
    tokens, gain, weight_q, weight_kv, gains, cosine, sine, idle,
    plain, query, query_raw, pair, key_raw,
):
    rows = tokens[...].astype(f32)
    scaled = rows * lax.rsqrt(jnp.mean(rows * rows, axis=-1, keepdims=True) + eps_norm)
    plain[...] = scaled.astype(bf16)
    normed = (scaled * gain[...]).astype(bf16)

    def head(raw, head_gain):
        scale = lax.rsqrt(jnp.mean(raw * raw, axis=-1, keepdims=True) + eps_norm)
        made = raw * scale * head_gain
        return (made * cosine[...] + turn(made) * sine[...]).astype(bf16)

    made = dot(normed, weight_kv[...])
    key_raw[...] = made[:, :KW]
    pair[:, :KW] = head(made[:, :KW], gains[1:2, :])
    pair[:, KW:] = made[:, KW:].astype(bf16)

    @pl.when(pl.program_id(0) < 4)
    def _():
        made = dot(normed, weight_q[...])
        query_raw[...] = made
        for h in range(2):
            cols = slice(h * HEAD_SIZE, (h + 1) * HEAD_SIZE)
            query[:, cols] = head(made[:, cols], gains[0:1, :])


def project(tokens, gain, weight_q, weight_kv, gains, cosine, sine, idle):
    def rows(width):
        return pl.BlockSpec((TILE, width), lambda t: (t, 0))

    def first(width):
        return pl.BlockSpec((TILE, width), lambda t: (jnp.minimum(t, 3), 0))

    def whole(v):
        return pl.BlockSpec(v.shape, lambda t: (0, 0))

    return pl.pallas_call(
        project_kernel,
        grid=(8,),
        out_shape=[
            jax.ShapeDtypeStruct((2048, D), bf16),
            jax.ShapeDtypeStruct((1024, QW), bf16),
            jax.ShapeDtypeStruct((1024, QW), f32),
            jax.ShapeDtypeStruct((2048, QW), bf16),
            jax.ShapeDtypeStruct((2048, KW), f32),
        ],
        in_specs=[
            rows(D), whole(gain), whole(weight_q), whole(weight_kv), whole(gains),
            rows(HEAD_SIZE), rows(HEAD_SIZE), pl.BlockSpec(memory_space=pl.ANY),
        ],
        out_specs=[rows(D), first(QW), first(QW), rows(QW), rows(KW)],
        compiler_params=pltpu.CompilerParams(vmem_limit_bytes=32 * 2**20),
        name="project",
    )(tokens, gain, weight_q, weight_kv, gains, cosine, sine, idle)


def mlp_kernel(
    near, far, backs, weight, down, normed, hidden, grad_gu, low, total
):
    step = pl.program_id(0)
    rows = jnp.where(step < 2, far[...], near[...])
    normed[...] = rows
    made = dot(rows, weight[...])
    gate = made[:, :FW]
    upper = made[:, FW:]
    sigma = jax.nn.sigmoid(gate)
    acted = gate * sigma
    hidden[...] = (acted * upper).astype(bf16)
    grad = dot(backs[...], down[...])
    grad_gu[:, :FW] = (grad * upper * sigma * (1.0 + gate * (1.0 - sigma))).astype(bf16)
    grad_gu[:, FW:] = (grad * acted).astype(bf16)
    part = dot(grad_gu[...], weight[...], contract_cols)

    @pl.when(step < 2)
    def _():
        low[...] = part.astype(bf16)

    @pl.when(step >= 2)
    def _():
        total[...] = part


def mlp(near, far, backs, weight, down):
    def rows(width):
        return pl.BlockSpec((TILE, width), lambda t: (lax.rem(t + 2, 4), 0))

    def early(width):
        return pl.BlockSpec((TILE, width), lambda t: (jnp.minimum(t, 1), 0))

    def late(width):
        return pl.BlockSpec((TILE, width), lambda t: (jnp.maximum(t - 2, 0), 0))

    def whole(v):
        return pl.BlockSpec(v.shape, lambda t: (0, 0))

    return pl.pallas_call(
        mlp_kernel,
        grid=(4,),
        out_shape=[
            jax.ShapeDtypeStruct((1024, D), bf16),
            jax.ShapeDtypeStruct((1024, FW), bf16),
            jax.ShapeDtypeStruct((1024, 2 * FW), bf16),
            jax.ShapeDtypeStruct((512, D), bf16),
            jax.ShapeDtypeStruct((512, D), f32),
        ],
        in_specs=[late(D), early(D), rows(D), whole(weight), whole(down)],
        out_specs=[rows(D), rows(FW), rows(2 * FW), early(D), late(D)],
        compiler_params=pltpu.CompilerParams(vmem_limit_bytes=40 * 2**20),
        name="mlp",
    )(near, far, backs, weight, down)


def attend(table, query, pair, *idle):
    return pl.pallas_call(
        lambda table, query, pair, *refs: attend_kernel(table, query, pair, *refs[len(idle) :]),
        out_shape=[
            jax.ShapeDtypeStruct((1024, QW), bf16),
            jax.ShapeDtypeStruct((16, 2 * BLK), f32),
        ],
        in_specs=[in_smem()]
        + [in_vmem()] * 2
        + [pl.BlockSpec(memory_space=pl.ANY)] * len(idle),
        out_specs=[in_vmem()] * 2,
        scratch_shapes=[
            pltpu.VMEM((2048, HEAD_SIZE), bf16),
            pltpu.VMEM((2048, HEAD_SIZE), bf16),
            pltpu.VMEM((HEAD_SIZE, 2048), bf16),
        ],
        compiler_params=pltpu.CompilerParams(vmem_limit_bytes=48 * 2**20),
        cost_estimate=pl.CostEstimate(flops=1000000, bytes_accessed=100000, transcendentals=0),
        name="attend",
    )(table, query, pair, *idle)


def attend_back(*args):
    return pl.pallas_call(
        attend_back_kernel,
        out_shape=[
            jax.ShapeDtypeStruct((1024, 3 * QW + 128), bf16),
            jax.ShapeDtypeStruct((1024, QW), bf16),
            jax.ShapeDtypeStruct((1024, QW), f32),
            jax.ShapeDtypeStruct((1024, QW), bf16),
        ],
        in_specs=[in_smem()]
        + [in_vmem()] * (len(args) - 2)
        + [pl.BlockSpec(memory_space=pl.ANY)],
        out_specs=[in_vmem()] * 4,
        scratch_shapes=[
            pltpu.VMEM((2048, HEAD_SIZE), bf16),
            pltpu.VMEM((2048, HEAD_SIZE), bf16),
            pltpu.VMEM((HEAD_SIZE, 2048), bf16),
            pltpu.VMEM((2048, HEAD_SIZE), f32),
            pltpu.VMEM((2048, HEAD_SIZE), f32),
            pltpu.VMEM((1024, QW), f32),
            pltpu.VMEM((1024, QW), f32),
            pltpu.VMEM((1024, QW), f32),
            pltpu.VMEM((1024, QW), bf16),
        ],
        compiler_params=pltpu.CompilerParams(vmem_limit_bytes=48 * 2**20),
        cost_estimate=pl.CostEstimate(
            flops=3100000000, bytes_accessed=6000000, transcendentals=2400000
        ),
        name="attend_back",
    )(*args)


def collect_kernel(got, mlp, weights, own_gain, share, stats):
    total = got[0:64, :].astype(f32)
    for k in range(1, 16):
        total = total + got[64 * k : 64 * k + 64, :].astype(f32)
    gain_sum = total[0:1, 3 * QW :] + total[1:2, 3 * QW :]
    squares = jnp.zeros((8, HEAD_SIZE), f32)
    for j in range(1, 8):
        gain_sum = gain_sum + total[8 * j : 8 * j + 1, 3 * QW :]
        gain_sum = gain_sum + total[8 * j + 1 : 8 * j + 2, 3 * QW :]
    gain_part = jnp.zeros((8, HEAD_SIZE), f32)
    gain = own_gain[...]
    at_mlp = QKVC + 8 * QW

    def fold(v):
        made = v[:, :HEAD_SIZE]
        for k in range(1, v.shape[1] // HEAD_SIZE):
            made = made + v[:, k * HEAD_SIZE : (k + 1) * HEAD_SIZE]
        return made

    for j in range(8):
        rows = slice(8 * j, 8 * j + 8)
        for at, width, base in ((0, QW, 0), (QW, KW, 2048), (QW + KW, KW, 3072)):
            spot = slice(base + j * width, base + (j + 1) * width)
            plain = total[rows, at : at + width]
            gain_part = gain_part + fold(plain * weights[:, spot].astype(f32))
            made = plain * gain
            share[:, spot] = made
            squares = squares + fold(made * made)
        made = total[rows, 2 * QW : 3 * QW]
        share[:, QKVC + j * QW : QKVC + (j + 1) * QW] = made
        squares = squares + fold(made * made)
        for part in range(3):
            made = mlp[rows, part * FW : (part + 1) * FW]
            first = at_mlp + part * FF + j * FW
            share[:, first : first + FW] = made
            squares = squares + fold(made * made)
    attn = jnp.sum(gain_part, axis=1, keepdims=True)
    whole = jnp.sum(squares) + jnp.sum(gain_sum * gain_sum) + jnp.sum(attn * attn)
    row = lax.broadcasted_iota(jnp.int32, (8, HEAD_SIZE), 0)
    lane = lax.broadcasted_iota(jnp.int32, (8, HEAD_SIZE), 1)
    own_attn = jnp.sum(jnp.where(lane == row, attn, 0.0), axis=0, keepdims=True)
    first = lax.broadcasted_iota(jnp.int32, (1, HEAD_SIZE), 1)
    stats[:, :HEAD_SIZE] = gain_sum
    stats[:, HEAD_SIZE:] = jnp.where(first == 8, whole, own_attn)


def collect(got, mlp, weights, own_gain):
    return pl.pallas_call(
        collect_kernel,
        out_shape=[
            jax.ShapeDtypeStruct((8, 15360), f32),
            jax.ShapeDtypeStruct((1, 2 * HEAD_SIZE), f32),
        ],
        in_specs=[in_vmem()] * 4,
        out_specs=[in_vmem()] * 2,
        compiler_params=pltpu.CompilerParams(vmem_limit_bytes=32 * 2**20),
        name="collect",
    )(got, mlp, weights, own_gain)


def slot_places(positions):
    seq = lax.axis_index("ylo") * 4 + lax.axis_index("z")
    table = lax.dynamic_index_in_dim(positions, seq, 0, keepdims=False).reshape(2, 4, 2, 128)
    xi = lax.axis_index("x")
    table = lax.dynamic_slice_in_dim(jnp.concatenate([table, table], axis=1), xi, 4, axis=1)
    table = jnp.transpose(table, (0, 2, 1, 3))
    table = jnp.where(lax.axis_index("core") == 0, table, table[:, ::-1])
    table = jnp.where(lax.axis_index("yhi") == 0, table, table[::-1])
    return table.reshape(2048)


def body(
    tokens,
    cotangent,
    positions,
    weights,
    norm_gains,
    moment_weights,
    second_weights,
    moment_gains,
    second_gains,
):
    o_q, o_k, o_v, o_o = 0, 2048, 3072, 4096
    o_g, o_u, o_d = 6144, 6144 + FF, 6144 + 2 * FF
    w_q = weights[:, o_q:o_k].reshape(8, 8, QW)
    w_k = weights[:, o_k:o_v].reshape(8, 8, KW)
    w_v = weights[:, o_v:o_o].reshape(8, 8, KW)
    w_o = weights[:, o_o:o_g].reshape(8, 8, QW)
    w_g = weights[:, o_g:o_u].reshape(8, 8, FW)
    w_u = weights[:, o_u:o_d].reshape(8, 8, FW)
    w_d = weights[:, o_d:].reshape(8, 8, FW)
    rank = lax.axis_index("ylo")
    for name, size in (("z", 4), ("yhi", 2), ("x", 4), ("core", 2)):
        rank = rank * size + lax.axis_index(name)
    own = tokens[0].astype(f32)
    own_back = cotangent[0].astype(f32)

    w_gains = jnp.pad(norm_gains.reshape(1, 1, 18), ((0, 7), (0, 0), (0, 110)))
    sent = to_all(jnp.concatenate([w_q, w_k, w_v, w_o, jnp.broadcast_to(w_gains, (8, 8, 128))], axis=2))
    w_first = lax.all_to_all(sent, ALL, 0, 0, tiled=True)
    both = jnp.stack([tokens[0], swap_yhi(tokens[0])]).reshape(256, D)
    near = near_gather(both)
    tokens_all = jnp.transpose(
        jnp.concatenate([near, swap_core(near)], axis=0).reshape(8, 2, 128, D), (1, 0, 2, 3)
    ).reshape(2048, D)
    rest = to_owners(jnp.concatenate([w_g, w_u, w_d], axis=2))
    rest = lax.all_to_all(rest, GROUP, 0, 0, tiled=True)
    rest_sent = jnp.broadcast_to(rest[None], (16, 64, 3 * FW)).reshape(1024, 3 * FW)
    table = slot_places(positions)[::BLK] // BLK
    cosine, sine = turn_tables(table)

    w_qkv = w_first[:, : 2 * QW]
    w_out = w_first[:, 2 * QW : 3 * QW]
    gain_all = w_first[:, 3 * QW :].reshape(128, 8, 128)[:, 0, :18].reshape(2304).astype(f32)
    gain_attn = gain_all[:D]
    gain_mlp = gain_all[D : 2 * D]
    head_gains = gain_all[2 * D :].reshape(2, HEAD_SIZE)
    plain, query, query_raw, pair, key_raw = project(
        tokens_all, gain_attn[None], w_first[:, :QW], w_first[:, QW : 2 * QW],
        head_gains, cosine, sine, rest_sent,
    )
    w_rest = lax.all_to_all(rest_sent, PLANE, 0, 0, tiled=True)
    w_gateup = w_rest[:, : 2 * FW]
    w_down = w_rest[:, 2 * FW :]
    backs_low = group_gather(cotangent[0])
    attended, logsum = attend(table, query, pair, backs_low)

    middle = own + group_scatter(attended, w_out, contract_cols)
    scale_two = rms_scale(middle)
    normed_two = near_gather((middle * scale_two * gain_mlp).astype(bf16))
    normed_two = after(normed_two, w_rest)
    normed_all, hidden, grad_gu, low, total = mlp(
        normed_two, swap_core(normed_two), backs_low, w_gateup, w_down
    )
    grad_normed_two = group_fold(total, low)
    term_mlp = jnp.concatenate(
        [dot(normed_all, grad_gu, contract_rows), dot(backs_low, hidden, contract_rows)], axis=1
    )
    plane_mlp = plane_sum(term_mlp)

    grad_mid_part, gain_mlp_grad = norm_back(middle, scale_two, gain_mlp, grad_normed_two)
    grad_mid = own_back + grad_mid_part
    mid_near = near_gather(grad_mid.astype(bf16))
    last, grad_q_low, grad_pair, grad_pair_away = attend_back(
        table, query, pair, attended, logsum, query_raw, key_raw, cosine, sine, head_gains,
        gain_mlp_grad.reshape(8, HEAD_SIZE), plain, mid_near, swap_core(mid_near), w_out, plane_mlp,
    )
    got = lax.all_to_all(last, ALL, 0, 0, tiled=True)
    share_mlp = lax.all_to_all(after(plane_mlp, last), GROUP, 0, 0, tiled=True)
    own_gain = lax.dynamic_slice_in_dim(gain_attn, rank * 8, 8)
    grad_share, stats = collect(got, share_mlp, weights, own_gain[:, None])
    shared = lax.all_to_all(
        jnp.broadcast_to(stats, (128, 2 * HEAD_SIZE)), ALL, 0, 0, tiled=True
    )

    output = middle + group_scatter(hidden, w_down, contract_cols)
    grad_pair_sum = grad_pair + swap_yhi(grad_pair_away).astype(f32)
    grad_key = grad_pair_sum[:, :KW]
    grad_key = grad_key * cosine[:1024] - jnp.roll(grad_key, HEAD_SIZE // 2, axis=1) * sine[:1024]
    key_near = key_raw[:1024]
    grad_key_raw, _ = norm_back(key_near, rms_scale(key_near), head_gains[1], grad_key)
    grad_proj = jnp.concatenate(
        [grad_q_low, grad_key_raw.astype(bf16), grad_pair_sum[:, KW:].astype(bf16)], axis=1
    )
    grad_normed = group_scatter(grad_proj, w_qkv, contract_cols)
    grad_in_part, _ = norm_back(own, rms_scale(own), gain_attn, grad_normed)
    grad_inputs = grad_mid + grad_in_part

    norm_all = jnp.sqrt(jnp.sum(shared[:, HEAD_SIZE + 8]))
    gain_whole = jnp.concatenate(
        [shared[:, HEAD_SIZE : HEAD_SIZE + 8].reshape(D), shared[:10, :HEAD_SIZE].reshape(1280)]
    )
    gain_grad = lax.dynamic_slice_in_dim(gain_whole, rank * 18, 18)
    factor = jnp.minimum(1.0, clip_limit / (norm_all + 1e-06))
    column = jnp.arange(grad_share.shape[1])
    rates = jnp.where(
        (column >= QKVC) & (column < QKVC + QUERY_HEADS * HEAD_SIZE), rate_output, rate_matrix
    )
    new_w, new_mw, new_vw = adam(
        weights.astype(f32),
        grad_share * factor,
        moment_weights,
        second_weights,
        rates[None, :],
        decay_rate,
    )
    new_g, new_mg, new_vg = adam(
        norm_gains.astype(f32),
        gain_grad * factor,
        moment_gains,
        second_gains,
        rate_gain,
        0.0,
    )
    return (
        output[None],
        grad_inputs[None],
        norm_all.reshape(1),
        new_w,
        new_mw,
        new_vw,
        new_g,
        new_mg,
        new_vg,
    )


def solution(mesh):
    parts = Mesh(mesh.devices.reshape(2, 4, 2, 4, 2), ALL)
    rows = P(("ylo", "z"), ("yhi", "x", "core"), None)
    owned = P(ALL, None)
    small = P(ALL)
    return jax.shard_map(
        body,
        mesh=parts,
        in_specs=(rows, rows, P(), owned, small, owned, owned, small, small),
        out_specs=(rows, rows, P(), owned, owned, owned, small, small, small),
        check_vma=False,
    )
```

time: 450 us -> 376 us (0.84); the launches traced: 442 us -> 376 us
  matrix products: 95.1 us -> 20.8 us
  Pallas kernels: 0 us -> 55 us
  other arithmetic: 54.4 us -> 24.1 us
  waiting for transfers between devices: 143 us -> 122 us
  blocking collectives: 0 us -> 11.1 us
  starting transfers between devices: 106 us -> 100 us
    dot_general x30 -> x8, matrix products: 95.1 us -> 20.8 us  [dot(): return lax.dot_general(a, b, dims, preferred_element_type=f32)]
    pallas_call x0 -> x7, Pallas kernels: none -> 55 us  [the longest x1 29.7 us: attend_back(): pl.pallas_call(attend_back_kernel, out_shape=[jax.ShapeDtypeStruct((1024,...]
    all_to_all x8 -> x6, waiting for transfers between devices: 47.5 us -> 15.1 us  [the longest x1 7.93 us: body(): got = lax.all_to_all(last, ALL, 0, 0, tiled=True)]
    all_to_all x8 -> x6, starting transfers between devices: 62.4 us -> 41.6 us  [the longest x1 11.2 us: body(): w_first = lax.all_to_all(sent, ALL, 0, 0, tiled=True)]
    ppermute x24, waiting for transfers between devices: 57.9 us -> 72.3 us  [shift_x(): return lax.ppermute(v, 'x', [(i, (i + k) % 4) for i in range(4)])]
    convert_element_type x4 -> x5, other arithmetic: 13.9 us -> 1.13 us  [the longest x1 0.43 us: group_fold(): low = near.astype(bf16)]
    ppermute x8, starting transfers between devices: 10.3 us -> 21.7 us  [swap_core(): return lax.ppermute(v, 'core', [(0, 1), (1, 0)])]
    all_to_all x0 -> x1, blocking collectives: none -> 11.1 us  [body(): share_mlp = lax.all_to_all(after(plane_mlp, last), GROUP, 0, 0, tiled=True)]
  transfers between devices with their start and end apart: 42 -> 40, of which waited for: 21 -> 16; matrix products, arithmetic and copies ran while one was open for 36% -> 16% of each run, Pallas kernels for 0% -> 0%
where the time goes in v2:
time: 376 us
  waiting for transfers between devices  122 us (32%)
  starting transfers between devices  100 us (27%)
  Pallas kernels  55 us (15%)
  local copies, waits for them, and re-layouts  39.4 us (10%)
  other arithmetic  24.1 us (6%)
  matrix products  20.8 us (6%)
  blocking collectives  11.1 us (3%)
    ppermute x24, waiting for transfers between devices, shift_x(): return lax.ppermute(v, 'x', [(i, (i + k) % 4) for i in range(4)])  72.3 us
    ppermute x2, waiting for transfers between devices, swap_yhi(): return lax.ppermute(v, 'yhi', [(0, 1), (1, 0)])  34.2 us
    ppermute x24, starting transfers between devices, shift_x(): return lax.ppermute(v, 'x', [(i, (i + k) % 4) for i in range(4)])  30.1 us
    pallas_call x1, Pallas kernels, attend_back(): pl.pallas_call(attend_back_kernel, out_shape=[jax.ShapeDtypeStruct((1024,...  29.7 us
    ppermute x8, starting transfers between devices, swap_core(): return lax.ppermute(v, 'core', [(0, 1), (1, 0)])  21.7 us
    dot_general x8, matrix products, dot(): return lax.dot_general(a, b, dims, preferred_element_type=f32)  20.8 us
    unnamed x107, local copies, waits for them, and re-layouts  15 us
    pallas_call x1, Pallas kernels, attend(): pl.pallas_call(lambda table, query, pair, *refs: attend_kernel(table, que...  12.6 us
  transfers between devices with their start and end apart: 40, of which 16 were waited for; matrix products, arithmetic and copies ran while one was open for 16% of the time, Pallas kernels for 0%

profile of v2, /device:TPU:1, one launch (start us, length us, event | category | flops | bytes accessed | tf_op | source)
XLA Modules:
  0.0 376.1 jit_solution(18390367719788423167)
XLA Ops:
  0.7 3.4 collective-permute-start.5
  9.6 11.2 %all-to-all-start = ((bf16[128,8,896]{2,1,0:T(8,128)(2,1)}), bf16[128,8,896]{2,1,0:T(8,128)(2,1)}, u32[]{:S(2)}, u32[]{:S(2)}) async-start(bf16[128,8,896]{2,1,0:T(8,128)(2,1)} %bitcast.16), calls=%async_computation | async-start | bytes 3670016 | tf_op jit(solution)/shard_map/all_to_all | solution.py:626
  20.8 3.0 collective-permute-start
  25.5 23.5 %collective-permute-done = bf16[128,1024]{1,0:T(8,128)(2,1)S(1)} collective-permute-done((bf16[128,1024]{1,0:T(8,128)(2,1)S(1)}, bf16[128,1024]{1,0:T(8,128)(2,1)S(1)}, u32[]{:S(2)}, u32[]{:S(2)}) %collective-permute-start) | collective-permute-done | bytes 262176 | tf_op jit(solution)/shard_map/ppermute | solution.py:84
  49.0 2.4 collective-permute-start.1
  56.6 6.2 %collective-permute-done.1 = bf16[256,1024]{1,0:T(8,128)(2,1)S(1)} collective-permute-done((bf16[256,1024]{1,0:T(8,128)(2,1)S(1)}, bf16[256,1024]{1,0:T(8,128)(2,1)S(1)}, u32[]{:S(2)}, u32[]{:S(2)}) %collective-permute-start.1) | collective-permute-done | bytes 524320 | tf_op jit(solution)/shard_map/ppermute | solution.py:88
  62.8 2.6 collective-permute-done.2
  65.4 12.6 %collective-permute-done.3 = bf16[256,1024]{1,0:T(8,128)(2,1)S(1)} collective-permute-done((bf16[256,1024]{1,0:T(8,128)(2,1)S(1)}, bf16[256,1024]{1,0:T(8,128)(2,1)S(1)}, u32[]{:S(2)}, u32[]{:S(2)}) %collective-permute-start.3) | collective-permute-done | bytes 524320 | tf_op jit(solution)/shard_map/ppermute | solution.py:88
  85.0 4.3 %all-to-all-start.1 = ((bf16[8,8,1152]{2,1,0:T(8,128)(2,1)}), bf16[8,8,1152]{2,1,0:T(8,128)(2,1)}, u32[]{:S(2)}, u32[]{:S(2)}) async-start(bf16[8,8,1152]{2,1,0:T(8,128)(2,1)} %maximum_bitcast_fusion), calls=%async_computation.1 | async-start | bytes 294912 | tf_op jit(solution)/shard_map/all_to_all | solution.py:633
  90.7 2.6 fusion.52
  93.2 3.1 constant_dynamic-update-slice_fusion
  96.3 4.8 %copy.30 = bf16[8,2,128,1024]{3,2,0,1:T(8,128)(2,1)} copy(bf16[8,2,128,1024]{3,2,1,0:T(8,128)(2,1)} %bitcast.99) | data formatting | bytes 8388608 | tf_op jit(solution)/shard_map/reshape | solution.py:630
  101.1 2.8 broadcast_in_dim.84
  103.9 2.2 copy-done.2
  106.1 6.5 %project.1 = (bf16[2048,1024]{1,0:T(8,128)(2,1)S(1)}, bf16[1024,256]{1,0:T(8,128)(2,1)S(1)}, f32[1024,256]{1,0:T(8,128)S(1)}, bf16[2048,256]{1,0:T(8,128)(2,1)S(1)}, f32[2048,128]{1,0:T(8,128)S(1)}) custom-call(bf16[2048,1024]{1,0:T(8,128)(2,1)S(1)} %bitcast.89, f32[1,1024]{1,0:T(1,128)S(1)} %bitcast.95, bf16[1024,256]{1,0:T(8,128)(2,1)S(1)} %copy-done.18, ...), custom_call_target="tpu_custom_call" | custom-call | tf_op jit(solution)/shard_map/project/pallas_call | solution.py:397
  116.7 12.6 %attend.1 = (bf16[1024,256]{1,0:T(8,128)(2,1)S(1)}, f32[16,128]{1,0:T(8,128)S(1)}) custom-call(s32[32]{0:T(128)S(1)} %get-tuple-element.72.table, bf16[1024,256]{1,0:T(8,128)(2,1)S(1)} %get-tuple-element.35.query, bf16[2048,256]{1,0:T(8,128)(2,1)S(1)} %get-tuple-element.36.pair, bf16[1024,1024]{1,0:T(8,128)(2,1)S(1)} %constant_dynamic-update-slice_fusion.10.refs_0_.backs), custom_call_target="tpu_custom_call" | custom-call | flops 1000000 | bytes 100000 | tf_op jit(solution)/shard_map/attend/pallas_call | solution.py:474
  129.3 2.6 convolution_convert_fusion.2
  131.9 5.2 %all-to-all-start.2 = ((bf16[16,64,1152]{2,1,0:T(8,128)(2,1)}), bf16[16,64,1152]{2,1,0:T(8,128)(2,1)}, u32[]{:S(2)}, u32[]{:S(2)}) async-start(bf16[16,64,1152]{2,1,0:T(8,128)(2,1)} %broadcast_in_dim.84), calls=%async_computation.2 | async-start | bytes 4718592 | tf_op jit(solution)/shard_map/all_to_all | solution.py:648
  139.1 3.0 collective-permute-start.12
  143.3 9.5 %collective-permute-done.12 = bf16[128,1024]{1,0:T(8,128)(2,1)S(1)} collective-permute-done((bf16[128,1024]{1,0:T(8,128)(2,1)S(1)}, bf16[128,1024]{1,0:T(8,128)(2,1)S(1)}, u32[]{:S(2)}, u32[]{:S(2)}) %collective-permute-start.12) | collective-permute-done | bytes 262176 | tf_op jit(solution)/shard_map/ppermute | solution.py:88
  152.8 4.8 %collective-permute-done.10 = bf16[128,1024]{1,0:T(8,128)(2,1)S(1)} collective-permute-done((bf16[128,1024]{1,0:T(8,128)(2,1)S(1)}, bf16[128,1024]{1,0:T(8,128)(2,1)S(1)}, u32[]{:S(2)}, u32[]{:S(2)}) %collective-permute-start.10) | collective-permute-done | bytes 262176 | tf_op jit(solution)/shard_map/ppermute | solution.py:88
  158.7 2.0 collective-permute-start.13
  160.8 11.6 %collective-permute-done.15 = bf16[128,1024]{1,0:T(8,128)(2,1)S(1)} collective-permute-done((bf16[128,1024]{1,0:T(8,128)(2,1)S(1)}, bf16[128,1024]{1,0:T(8,128)(2,1)S(1)}, u32[]{:S(2)}, u32[]{:S(2)}) %collective-permute-start.15) | collective-permute-done | bytes 262176 | tf_op jit(solution)/shard_map/ppermute | solution.py:88
  178.2 5.8 %mlp.1 = (bf16[1024,1024]{1,0:T(8,128)(2,1)S(1)}, bf16[1024,384]{1,0:T(8,128)(2,1)S(1)}, bf16[1024,768]{1,0:T(8,128)(2,1)S(1)}, bf16[512,1024]{1,0:T(8,128)(2,1)S(1)}, f32[512,1024]{1,0:T(8,128)S(1)}) custom-call(bf16[512,1024]{1,0:T(8,128)(2,1)S(1)} %copy-done.6, bf16[512,1024]{1,0:T(8,128)(2,1)S(1)} %collective-permute-done.16.far, ...), custom_call_target="tpu_custom_call" | custom-call | tf_op jit(solution)/shard_map/mlp/pallas_call | solution.py:456
  184.0 13.1 %collective-permute-start.21 = (bf16[512,1024]{1,0:T(8,128)(2,1)S(1)}, bf16[512,1024]{1,0:T(8,128)(2,1)S(1)}, u32[]{:S(2)}, u32[]{:S(2)}) collective-permute-start(bf16[512,1024]{1,0:T(8,128)(2,1)S(1)} %get-tuple-element.40), channel_id=1, source_target_pairs={{0,1},{1,0},{2,3},{3,2},{4,5},{5,4},{6,7},{7,6},{8,9},{9,8},{10,11... | collective-permute-start | bytes 3145736 | tf_op jit(solution)/shard_map/ppermute | solution.py:80
  201.7 3.6 collective-permute-start.24
  208.2 6.2 %all-to-all-start.3 = ((bf16[16,64,1152]{2,1,0:T(8,128)(2,1)}), bf16[16,64,1152]{2,1,0:T(8,128)(2,1)}, u32[]{:S(2)}, u32[]{:S(2)}) async-start(bf16[16,64,1152]{2,1,0:T(8,128)(2,1)} %pad_maximum_fusion), calls=%async_computation.3 | async-start | bytes 4718592 | tf_op jit(solution)/shard_map/all_to_all | solution.py:155
  216.4 4.6 %collective-permute-done.22 = bf16[128,1024]{1,0:T(8,128)(2,1)} collective-permute-done((bf16[128,1024]{1,0:T(8,128)(2,1)}, bf16[128,1024]{1,0:T(8,128)(2,1)}, u32[]{:S(2)}, u32[]{:S(2)}) %collective-permute-start.22) | collective-permute-done | bytes 262176 | tf_op jit(solution)/shard_map/ppermute | solution.py:88
  223.8 2.0 collective-permute-start.25
  225.9 11.6 %collective-permute-done.27 = bf16[128,1024]{1,0:T(8,128)(2,1)S(1)} collective-permute-done((bf16[128,1024]{1,0:T(8,128)(2,1)S(1)}, bf16[128,1024]{1,0:T(8,128)(2,1)S(1)}, u32[]{:S(2)}, u32[]{:S(2)}) %collective-permute-start.27) | collective-permute-done | bytes 262176 | tf_op jit(solution)/shard_map/ppermute | solution.py:88
  240.4 7.2 %all-to-all-done.3 = bf16[16,64,1152]{2,1,0:T(8,128)(2,1)} async-done(((bf16[16,64,1152]{2,1,0:T(8,128)(2,1)}), bf16[16,64,1152]{2,1,0:T(8,128)(2,1)}, u32[]{:S(2)}, u32[]{:S(2)}) %all-to-all-start.3) | async-done | bytes 2359328 | tf_op jit(solution)/shard_map/all_to_all | solution.py:155
  247.6 2.1 convert_reduce_fusion.idle.refs_0_
  249.8 29.7 %attend_back.1 = (bf16[1024,896]{1,0:T(8,128)(2,1)}, bf16[1024,256]{1,0:T(8,128)(2,1)S(1)}, f32[1024,256]{1,0:T(8,128)S(1)}, bf16[1024,256]{1,0:T(8,128)(2,1)S(1)}) custom-call(s32[32]{0:T(128)S(1)} %get-tuple-element.72.table, bf16[1024,256]{1,0:T(8,128)(2,1)S(1)} %copy-done.16, bf16[2048,256]{1,0:T(8,128)(2,1)S(1)} %copy-done.12, ...), custom_call_target="tpu_custom_call" | custom-call | flops 3100000000 | bytes 6000000 | tf_op jit(solution)/shard_map/attend_back/pallas_call | solution.py:496
  279.5 3.9 %collective-permute-start.29 = (bf16[1024,256]{1,0:T(8,128)(2,1)S(1)}, bf16[1024,256]{1,0:T(8,128)(2,1)S(1)}, u32[]{:S(2)}, u32[]{:S(2)}) collective-permute-start(bf16[1024,256]{1,0:T(8,128)(2,1)S(1)} %get-tuple-element.49), channel_id=1, source_target_pairs={{0,8},{8,0},{1,9},{9,1},{2,10},{10,2},{3,11},{11,3},{4,12},{12,4},... | collective-permute-start | bytes 1572872 | tf_op jit(solution)/shard_map/ppermute | solution.py:84
  283.5 10.7 %collective-permute-done.29 = bf16[1024,256]{1,0:T(8,128)(2,1)S(1)} collective-permute-done((bf16[1024,256]{1,0:T(8,128)(2,1)S(1)}, bf16[1024,256]{1,0:T(8,128)(2,1)S(1)}, u32[]{:S(2)}, u32[]{:S(2)}) %collective-permute-start.29) | collective-permute-done | bytes 524320 | tf_op jit(solution)/shard_map/ppermute | solution.py:84
  297.5 2.9 convolution_convert_fusion.3
  300.4 2.1 collective-permute-start.30
  302.5 11.1 %all_to_all.63 = f32[8,8,1152]{2,1,0:T(8,128)S(1)} all-to-all(f32[8,8,1152]{2,1,0:T(8,128)} %bitcast.93), channel_id=1, replica_groups=mesh['ylo'=2,'z'=4,'yhi'=2,'x'=4,'core'=2] {'x','core'}, dimensions={0} | all-to-all | bytes 589824 | tf_op jit(solution)/shard_map/all_to_all | solution.py:675
  313.7 5.3 %all-to-all-start.4 = ((bf16[128,8,896]{2,1,0:T(8,128)(2,1)}), bf16[128,8,896]{2,1,0:T(8,128)(2,1)S(1)}, u32[]{:S(2)}, u32[]{:S(2)}) async-start(bf16[128,8,896]{2,1,0:T(8,128)(2,1)} %bitcast.98), calls=%async_computation.4 | async-start | bytes 3670016 | tf_op jit(solution)/shard_map/all_to_all | solution.py:674
  319.0 2.9 convolution_convert_fusion.1
  323.7 3.7 fusion.62
  331.4 3.6 fusion.63
  335.9 2.1 collective-permute-start.20
  339.2 7.9 %all-to-all-done.4 = bf16[128,8,896]{2,1,0:T(8,128)(2,1)S(1)} async-done(((bf16[128,8,896]{2,1,0:T(8,128)(2,1)}), bf16[128,8,896]{2,1,0:T(8,128)(2,1)S(1)}, u32[]{:S(2)}, u32[]{:S(2)}) %all-to-all-start.4) | async-done | bytes 1835040 | tf_op jit(solution)/shard_map/all_to_all | solution.py:674
  348.3 9.3 %all-to-all-start.6 = ((f32[128,1,256]{2,1,0:T(1,128)}), f32[128,1,256]{2,1,0:T(1,128)S(1)}, u32[]{:S(2)}, u32[]{:S(2)}) async-start(f32[128,1,256]{2,1,0:T(1,128)} %broadcast_in_dim.88), calls=%async_computation.6 | async-start | bytes 262144 | tf_op jit(solution)/shard_map/all_to_all | solution.py:678
  360.8 6.2 %collective-permute-done.18 = bf16[128,1024]{1,0:T(8,128)(2,1)S(1)} collective-permute-done((bf16[128,1024]{1,0:T(8,128)(2,1)}, bf16[128,1024]{1,0:T(8,128)(2,1)S(1)}, u32[]{:S(2)}, u32[]{:S(2)}) %collective-permute-start.18) | collective-permute-done | bytes 262176 | tf_op jit(solution)/shard_map/ppermute | solution.py:88
  367.0 3.1 fusion.11
  371.7 2.4 divide_subtract_fusion
  (230 shorter events, 66.8 us)
Async XLA Ops:
  0.7 51.1 %collective-permute-start.5 = (bf16[128,1024]{1,0:T(8,128)(2,1)}, bf16[128,1024]{1,0:T(8,128)(2,1)S(1)}, u32[]{:S(2)}, u32[]{:S(2)}) collective-permute-start(bf16[128,1024]{1,0:T(8,128)(2,1)} %bitcast.106), channel_id=1, source_target_pairs={{0,6},{2,0},{4,2},{6,4},{1,7},{3,1},{5,3},{7,5},{8,14},{10,8},{12,... | collective-permute-start | bytes 786440 | tf_op jit(solution)/shard_map/ppermute | solution.py:88
  4.0 49.6 %collective-permute-start.6 = (bf16[128,1024]{1,0:T(8,128)(2,1)}, bf16[128,1024]{1,0:T(8,128)(2,1)}, u32[]{:S(2)}, u32[]{:S(2)}) collective-permute-start(bf16[128,1024]{1,0:T(8,128)(2,1)} %bitcast.107), channel_id=1, source_target_pairs={{0,4},{2,6},{4,0},{6,2},{1,5},{3,7},{5,1},{7,3},{8,12},{10,14},{12... | collective-permute-start | bytes 786440 | tf_op jit(solution)/shard_map/ppermute | solution.py:88
  4.6 49.1 %collective-permute-start.7 = (bf16[128,1024]{1,0:T(8,128)(2,1)}, bf16[128,1024]{1,0:T(8,128)(2,1)}, u32[]{:S(2)}, u32[]{:S(2)}) collective-permute-start(bf16[128,1024]{1,0:T(8,128)(2,1)} %bitcast.108), channel_id=1, source_target_pairs={{0,2},{2,4},{4,6},{6,0},{1,3},{3,5},{5,7},{7,1},{8,10},{10,12},{12... | collective-permute-start | bytes 786440 | tf_op jit(solution)/shard_map/ppermute | solution.py:88
  9.6 75.4 %all-to-all-start = ((bf16[128,8,896]{2,1,0:T(8,128)(2,1)}), bf16[128,8,896]{2,1,0:T(8,128)(2,1)}, u32[]{:S(2)}, u32[]{:S(2)}) async-start(bf16[128,8,896]{2,1,0:T(8,128)(2,1)} %bitcast.16), calls=%async_computation | async-start | bytes 3670016 | tf_op jit(solution)/shard_map/all_to_all | solution.py:626
  20.8 28.2 %collective-permute-start = (bf16[128,1024]{1,0:T(8,128)(2,1)S(1)}, bf16[128,1024]{1,0:T(8,128)(2,1)S(1)}, u32[]{:S(2)}, u32[]{:S(2)}) collective-permute-start(bf16[128,1024]{1,0:T(8,128)(2,1)S(1)} %bitcast.105), channel_id=1, source_target_pairs={{0,8},{8,0},{1,9},{9,1},{2,10},{10,2},{3,11},{11,3},{4,12},{12,4},... | collective-permute-start | bytes 786440 | tf_op jit(solution)/shard_map/ppermute | solution.py:84
  25.4 27.1 %copy-start.25 = (f32[32,64,128]{2,1,0:T(8,128)}, f32[32,64,128]{2,1,0:T(8,128)S(1)}, u32[]{:S(2)}) copy-start(f32[32,64,128]{2,1,0:T(8,128)S(1)} %get-tuple-element.97) | copy-start | bytes 3145732
  25.4 78.5 %copy-start.3 = (f32[32,64,128]{2,1,0:T(8,128)}, f32[32,64,128]{2,1,0:T(8,128)S(1)}, u32[]{:S(2)}) copy-start(f32[32,64,128]{2,1,0:T(8,128)S(1)} %get-tuple-element.98) | copy-start | bytes 3145732
  25.4 28.2 %copy-start.33 = (bf16[1,128,1024]{2,1,0:T(8,128)(2,1)S(1)}, bf16[1,128,1024]{2,1,0:T(8,128)(2,1)}, u32[]{:S(2)}) copy-start(bf16[1,128,1024]{2,1,0:T(8,128)(2,1)} %param.10) | copy-start | bytes 786436
  49.0 13.7 %collective-permute-start.1 = (bf16[256,1024]{1,0:T(8,128)(2,1)S(1)}, bf16[256,1024]{1,0:T(8,128)(2,1)S(1)}, u32[]{:S(2)}, u32[]{:S(2)}) collective-permute-start(bf16[256,1024]{1,0:T(8,128)(2,1)S(1)} %bitcast.100), channel_id=1, source_target_pairs={{0,6},{2,0},{4,2},{6,4},{1,7},{3,1},{5,3},{7,5},{8,14},{10,8},{12,... | collective-permute-start | bytes 1572872 | tf_op jit(solution)/shard_map/ppermute | solution.py:88
  51.4 14.0 %collective-permute-start.2 = (bf16[256,1024]{1,0:T(8,128)(2,1)S(1)}, bf16[256,1024]{1,0:T(8,128)(2,1)S(1)}, u32[]{:S(2)}, u32[]{:S(2)}) collective-permute-start(bf16[256,1024]{1,0:T(8,128)(2,1)S(1)} %bitcast.101), channel_id=1, source_target_pairs={{0,4},{2,6},{4,0},{6,2},{1,5},{3,7},{5,1},{7,3},{8,12},{10,14},{12... | collective-permute-start | bytes 1572872 | tf_op jit(solution)/shard_map/ppermute | solution.py:88
  51.8 26.2 %collective-permute-start.3 = (bf16[256,1024]{1,0:T(8,128)(2,1)S(1)}, bf16[256,1024]{1,0:T(8,128)(2,1)S(1)}, u32[]{:S(2)}, u32[]{:S(2)}) collective-permute-start(bf16[256,1024]{1,0:T(8,128)(2,1)S(1)} %bitcast.102), channel_id=1, source_target_pairs={{0,2},{2,4},{4,6},{6,0},{1,3},{3,5},{5,7},{7,1},{8,10},{10,12},{12... | collective-permute-start | bytes 1572872 | tf_op jit(solution)/shard_map/ppermute | solution.py:88
  54.9 30.0 %collective-permute-start.8 = (bf16[512,1024]{1,0:T(8,128)(2,1)S(1)}, bf16[512,1024]{1,0:T(8,128)(2,1)S(1)}, u32[]{:S(2)}, u32[]{:S(2)}) collective-permute-start(bf16[512,1024]{1,0:T(8,128)(2,1)S(1)} %pad_maximum_fusion.2), channel_id=1, source_target_pairs={{0,1},{1,0},{2,3},{3,2},{4,5},{5,4},{6,7},{7,6},{8,9},{9,8},{10,11... | collective-permute-start | bytes 3145736 | tf_op jit(solution)/shard_map/ppermute | solution.py:80
  79.5 13.7 %collective-permute-start.4 = (bf16[1024,1024]{1,0:T(8,128)(2,1)}, bf16[1024,1024]{1,0:T(8,128)(2,1)}, u32[]{:S(2)}, u32[]{:S(2)}) collective-permute-start(bf16[1024,1024]{1,0:T(8,128)(2,1)} %pad_maximum_fusion.1), channel_id=1, source_target_pairs={{0,1},{1,0},{2,3},{3,2},{4,5},{5,4},{6,7},{7,6},{8,9},{9,8},{10,11... | collective-permute-start | bytes 6291464 | tf_op jit(solution)/shard_map/ppermute | solution.py:80
  85.0 16.2 %all-to-all-start.1 = ((bf16[8,8,1152]{2,1,0:T(8,128)(2,1)}), bf16[8,8,1152]{2,1,0:T(8,128)(2,1)}, u32[]{:S(2)}, u32[]{:S(2)}) async-start(bf16[8,8,1152]{2,1,0:T(8,128)(2,1)} %maximum_bitcast_fusion), calls=%async_computation.1 | async-start | bytes 294912 | tf_op jit(solution)/shard_map/all_to_all | solution.py:633
  131.8 5.3 %collective-permute-start.9 = (bf16[512,1024]{1,0:T(8,128)(2,1)}, bf16[512,1024]{1,0:T(8,128)(2,1)}, u32[]{:S(2)}, u32[]{:S(2)}) collective-permute-start(bf16[512,1024]{1,0:T(8,128)(2,1)} %convolution_convert_fusion.2), channel_id=1, source_target_pairs={{0,1},{1,0},{2,3},{3,2},{4,5},{5,4},{6,7},{7,6},{8,9},{9,8},{10,11... | collective-permute-start | bytes 3145736 | tf_op jit(solution)/shard_map/ppermute | solution.py:80
  131.9 42.0 %all-to-all-start.2 = ((bf16[16,64,1152]{2,1,0:T(8,128)(2,1)}), bf16[16,64,1152]{2,1,0:T(8,128)(2,1)}, u32[]{:S(2)}, u32[]{:S(2)}) async-start(bf16[16,64,1152]{2,1,0:T(8,128)(2,1)} %broadcast_in_dim.84), calls=%async_computation.2 | async-start | bytes 4718592 | tf_op jit(solution)/shard_map/all_to_all | solution.py:648
  139.1 13.7 %collective-permute-start.12 = (bf16[128,1024]{1,0:T(8,128)(2,1)S(1)}, bf16[128,1024]{1,0:T(8,128)(2,1)S(1)}, u32[]{:S(2)}, u32[]{:S(2)}) collective-permute-start(bf16[128,1024]{1,0:T(8,128)(2,1)S(1)} %get-tuple-element.88), channel_id=1, source_target_pairs={{0,6},{2,0},{4,2},{6,4},{1,7},{3,1},{5,3},{7,5},{8,14},{10,8},{12,... | collective-permute-start | bytes 786440 | tf_op jit(solution)/shard_map/ppermute | solution.py:88
  142.1 10.7 %collective-permute-start.11 = (bf16[128,1024]{1,0:T(8,128)(2,1)S(1)}, bf16[128,1024]{1,0:T(8,128)(2,1)S(1)}, u32[]{:S(2)}, u32[]{:S(2)}) collective-permute-start(bf16[128,1024]{1,0:T(8,128)(2,1)S(1)} %get-tuple-element.89), channel_id=1, source_target_pairs={{0,4},{2,6},{4,0},{6,2},{1,5},{3,7},{5,1},{7,3},{8,12},{10,14},{12... | collective-permute-start | bytes 786440 | tf_op jit(solution)/shard_map/ppermute | solution.py:88
  142.7 14.9 %collective-permute-start.10 = (bf16[128,1024]{1,0:T(8,128)(2,1)S(1)}, bf16[128,1024]{1,0:T(8,128)(2,1)S(1)}, u32[]{:S(2)}, u32[]{:S(2)}) collective-permute-start(bf16[128,1024]{1,0:T(8,128)(2,1)S(1)} %get-tuple-element.87), channel_id=1, source_target_pairs={{0,2},{2,4},{4,6},{6,0},{1,3},{3,5},{5,7},{7,1},{8,10},{10,12},{12... | collective-permute-start | bytes 786440 | tf_op jit(solution)/shard_map/ppermute | solution.py:88
  157.9 64.5 %copy-start.23 = (f32[128,1024]{1,0:T(8,128)}, f32[128,1024]{1,0:T(8,128)S(1)}, u32[]{:S(2)}) copy-start(f32[128,1024]{1,0:T(8,128)S(1)} %get-tuple-element.70) | copy-start | bytes 1572868
  158.0 14.4 %collective-permute-start.15 = (bf16[128,1024]{1,0:T(8,128)(2,1)S(1)}, bf16[128,1024]{1,0:T(8,128)(2,1)S(1)}, u32[]{:S(2)}, u32[]{:S(2)}) collective-permute-start(bf16[128,1024]{1,0:T(8,128)(2,1)S(1)} %multiply_convert_fusion), channel_id=1, source_target_pairs={{0,2},{2,4},{4,6},{6,0},{1,3},{3,5},{5,7},{7,1},{8,10},{10,12},{12... | collective-permute-start | bytes 786440 | tf_op jit(solution)/shard_map/ppermute | solution.py:88
  158.1 14.3 %collective-permute-start.14 = (bf16[128,1024]{1,0:T(8,128)(2,1)S(1)}, bf16[128,1024]{1,0:T(8,128)(2,1)S(1)}, u32[]{:S(2)}, u32[]{:S(2)}) collective-permute-start(bf16[128,1024]{1,0:T(8,128)(2,1)S(1)} %multiply_convert_fusion), channel_id=1, source_target_pairs={{0,4},{2,6},{4,0},{6,2},{1,5},{3,7},{5,1},{7,3},{8,12},{10,14},{12... | collective-permute-start | bytes 786440 | tf_op jit(solution)/shard_map/ppermute | solution.py:88
  158.7 14.0 %collective-permute-start.13 = (bf16[128,1024]{1,0:T(8,128)(2,1)S(1)}, bf16[128,1024]{1,0:T(8,128)(2,1)S(1)}, u32[]{:S(2)}, u32[]{:S(2)}) collective-permute-start(bf16[128,1024]{1,0:T(8,128)(2,1)S(1)} %multiply_convert_fusion), channel_id=1, source_target_pairs={{0,6},{2,0},{4,2},{6,4},{1,7},{3,1},{5,3},{7,5},{8,14},{10,8},{12,... | collective-permute-start | bytes 786440 | tf_op jit(solution)/shard_map/ppermute | solution.py:88
  173.9 4.3 %collective-permute-start.16 = (bf16[512,1024]{1,0:T(8,128)(2,1)}, bf16[512,1024]{1,0:T(8,128)(2,1)S(1)}, u32[]{:S(2)}, u32[]{:S(2)}) collective-permute-start(bf16[512,1024]{1,0:T(8,128)(2,1)} %after.2.near), channel_id=1, source_target_pairs={{0,1},{1,0},{2,3},{3,2},{4,5},{5,4},{6,7},{7,6},{8,9},{9,8},{10,11... | collective-permute-start | bytes 3145736 | tf_op jit(solution)/shard_map/ppermute | solution.py:80
  184.0 16.4 %collective-permute-start.21 = (bf16[512,1024]{1,0:T(8,128)(2,1)S(1)}, bf16[512,1024]{1,0:T(8,128)(2,1)S(1)}, u32[]{:S(2)}, u32[]{:S(2)}) collective-permute-start(bf16[512,1024]{1,0:T(8,128)(2,1)S(1)} %get-tuple-element.40), channel_id=1, source_target_pairs={{0,1},{1,0},{2,3},{3,2},{4,5},{5,4},{6,7},{7,6},{8,9},{9,8},{10,11... | collective-permute-start | bytes 3145736 | tf_op jit(solution)/shard_map/ppermute | solution.py:80
  201.7 14.7 %collective-permute-start.24 = (bf16[128,1024]{1,0:T(8,128)(2,1)}, bf16[128,1024]{1,0:T(8,128)(2,1)}, u32[]{:S(2)}, u32[]{:S(2)}) collective-permute-start(bf16[128,1024]{1,0:T(8,128)(2,1)} %get-tuple-element.82), channel_id=1, source_target_pairs={{0,6},{2,0},{4,2},{6,4},{1,7},{3,1},{5,3},{7,5},{8,14},{10,8},{12,... | collective-permute-start | bytes 786440 | tf_op jit(solution)/shard_map/ppermute | solution.py:88
  205.3 11.1 %collective-permute-start.23 = (bf16[128,1024]{1,0:T(8,128)(2,1)}, bf16[128,1024]{1,0:T(8,128)(2,1)}, u32[]{:S(2)}, u32[]{:S(2)}) collective-permute-start(bf16[128,1024]{1,0:T(8,128)(2,1)} %get-tuple-element.83), channel_id=1, source_target_pairs={{0,4},{2,6},{4,0},{6,2},{1,5},{3,7},{5,1},{7,3},{8,12},{10,14},{12... | collective-permute-start | bytes 786440 | tf_op jit(solution)/shard_map/ppermute | solution.py:88
  205.9 15.1 %collective-permute-start.22 = (bf16[128,1024]{1,0:T(8,128)(2,1)}, bf16[128,1024]{1,0:T(8,128)(2,1)}, u32[]{:S(2)}, u32[]{:S(2)}) collective-permute-start(bf16[128,1024]{1,0:T(8,128)(2,1)} %get-tuple-element.81), channel_id=1, source_target_pairs={{0,2},{2,4},{4,6},{6,0},{1,3},{3,5},{5,7},{7,1},{8,10},{10,12},{12... | collective-permute-start | bytes 786440 | tf_op jit(solution)/shard_map/ppermute | solution.py:88
  208.2 39.4 %all-to-all-start.3 = ((bf16[16,64,1152]{2,1,0:T(8,128)(2,1)}), bf16[16,64,1152]{2,1,0:T(8,128)(2,1)}, u32[]{:S(2)}, u32[]{:S(2)}) async-start(bf16[16,64,1152]{2,1,0:T(8,128)(2,1)} %pad_maximum_fusion), calls=%async_computation.3 | async-start | bytes 4718592 | tf_op jit(solution)/shard_map/all_to_all | solution.py:155
  223.2 26.5 %copy-start.16 = (bf16[1024,256]{1,0:T(8,128)(2,1)S(1)}, bf16[1024,256]{1,0:T(8,128)(2,1)}, u32[]{:S(2)}) copy-start(bf16[1024,256]{1,0:T(8,128)(2,1)} %copy-done.15) | copy-start | bytes 1572868
  223.2 14.3 %collective-permute-start.27 = (bf16[128,1024]{1,0:T(8,128)(2,1)S(1)}, bf16[128,1024]{1,0:T(8,128)(2,1)S(1)}, u32[]{:S(2)}, u32[]{:S(2)}) collective-permute-start(bf16[128,1024]{1,0:T(8,128)(2,1)S(1)} %fusion.46), channel_id=1, source_target_pairs={{0,2},{2,4},{4,6},{6,0},{1,3},{3,5},{5,7},{7,1},{8,10},{10,12},{12... | collective-permute-start | bytes 786440 | tf_op jit(solution)/shard_map/ppermute | solution.py:88
  223.2 14.3 %collective-permute-start.26 = (bf16[128,1024]{1,0:T(8,128)(2,1)S(1)}, bf16[128,1024]{1,0:T(8,128)(2,1)S(1)}, u32[]{:S(2)}, u32[]{:S(2)}) collective-permute-start(bf16[128,1024]{1,0:T(8,128)(2,1)S(1)} %fusion.46), channel_id=1, source_target_pairs={{0,4},{2,6},{4,0},{6,2},{1,5},{3,7},{5,1},{7,3},{8,12},{10,14},{12... | collective-permute-start | bytes 786440 | tf_op jit(solution)/shard_map/ppermute | solution.py:88
  223.8 14.0 %collective-permute-start.25 = (bf16[128,1024]{1,0:T(8,128)(2,1)S(1)}, bf16[128,1024]{1,0:T(8,128)(2,1)S(1)}, u32[]{:S(2)}, u32[]{:S(2)}) collective-permute-start(bf16[128,1024]{1,0:T(8,128)(2,1)S(1)} %fusion.46), channel_id=1, source_target_pairs={{0,6},{2,0},{4,2},{6,4},{1,7},{3,1},{5,3},{7,5},{8,14},{10,8},{12,... | collective-permute-start | bytes 786440 | tf_op jit(solution)/shard_map/ppermute | solution.py:88
  238.9 10.8 %collective-permute-start.28 = (bf16[512,1024]{1,0:T(8,128)(2,1)}, bf16[512,1024]{1,0:T(8,128)(2,1)}, u32[]{:S(2)}, u32[]{:S(2)}) collective-permute-start(bf16[512,1024]{1,0:T(8,128)(2,1)} %pad_maximum_fusion.4.mid_near), channel_id=1, source_target_pairs={{0,1},{1,0},{2,3},{3,2},{4,5},{5,4},{6,7},{7,6},{8,9},{9,8},{10,11... | collective-permute-start | bytes 3145736 | tf_op jit(solution)/shard_map/ppermute | solution.py:80
  249.7 29.8 %copy-start.7 = (f32[64,1152]{1,0:T(8,128)}, f32[64,1152]{1,0:T(8,128)S(1)}, u32[]{:S(2)}) copy-start(f32[64,1152]{1,0:T(8,128)S(1)} %convert_reduce_fusion.idle.refs_0_) | copy-start | bytes 884740
  249.7 33.7 %copy-start.4 = (f32[32,64,128]{2,1,0:T(8,128)S(1)}, f32[32,64,128]{2,1,0:T(8,128)}, u32[]{:S(2)}) copy-start(f32[32,64,128]{2,1,0:T(8,128)} %copy-done.3) | copy-start | bytes 3145732
  249.8 33.7 %copy-start.26 = (f32[32,64,128]{2,1,0:T(8,128)S(1)}, f32[32,64,128]{2,1,0:T(8,128)}, u32[]{:S(2)}) copy-start(f32[32,64,128]{2,1,0:T(8,128)} %copy-done.25) | copy-start | bytes 3145732
  279.5 14.7 %collective-permute-start.29 = (bf16[1024,256]{1,0:T(8,128)(2,1)S(1)}, bf16[1024,256]{1,0:T(8,128)(2,1)S(1)}, u32[]{:S(2)}, u32[]{:S(2)}) collective-permute-start(bf16[1024,256]{1,0:T(8,128)(2,1)S(1)} %get-tuple-element.49), channel_id=1, source_target_pairs={{0,8},{8,0},{1,9},{9,1},{2,10},{10,2},{3,11},{11,3},{4,12},{12,4},... | collective-permute-start | bytes 1572872 | tf_op jit(solution)/shard_map/ppermute | solution.py:84
  300.4 23.3 %collective-permute-start.30 = (bf16[512,1024]{1,0:T(8,128)(2,1)}, bf16[512,1024]{1,0:T(8,128)(2,1)}, u32[]{:S(2)}, u32[]{:S(2)}) collective-permute-start(bf16[512,1024]{1,0:T(8,128)(2,1)} %convolution_convert_fusion.3), channel_id=1, source_target_pairs={{0,1},{1,0},{2,3},{3,2},{4,5},{5,4},{6,7},{7,6},{8,9},{9,8},{10,11... | collective-permute-start | bytes 3145736 | tf_op jit(solution)/shard_map/ppermute | solution.py:80
  313.7 33.4 %all-to-all-start.4 = ((bf16[128,8,896]{2,1,0:T(8,128)(2,1)}), bf16[128,8,896]{2,1,0:T(8,128)(2,1)S(1)}, u32[]{:S(2)}, u32[]{:S(2)}) async-start(bf16[128,8,896]{2,1,0:T(8,128)(2,1)} %bitcast.98), calls=%async_computation.4 | async-start | bytes 3670016 | tf_op jit(solution)/shard_map/all_to_all | solution.py:674
  321.8 9.5 %collective-permute-start.17 = (bf16[512,1024]{1,0:T(8,128)(2,1)}, bf16[512,1024]{1,0:T(8,128)(2,1)}, u32[]{:S(2)}, u32[]{:S(2)}) collective-permute-start(bf16[512,1024]{1,0:T(8,128)(2,1)} %convolution_convert_fusion.1), channel_id=1, source_target_pairs={{0,1},{1,0},{2,3},{3,2},{4,5},{5,4},{6,7},{7,6},{8,9},{9,8},{10,11... | collective-permute-start | bytes 3145736 | tf_op jit(solution)/shard_map/ppermute | solution.py:80
  328.3 29.3 %collective-permute-start.33 = (bf16[128,1024]{1,0:T(8,128)(2,1)}, bf16[128,1024]{1,0:T(8,128)(2,1)}, u32[]{:S(2)}, u32[]{:S(2)}) collective-permute-start(bf16[128,1024]{1,0:T(8,128)(2,1)} %get-tuple-element.77), channel_id=1, source_target_pairs={{0,6},{2,0},{4,2},{6,4},{1,7},{3,1},{5,3},{7,5},{8,14},{10,8},{12,... | collective-permute-start | bytes 786440 | tf_op jit(solution)/shard_map/ppermute | solution.py:88
  330.2 28.8 %collective-permute-start.32 = (bf16[128,1024]{1,0:T(8,128)(2,1)}, bf16[128,1024]{1,0:T(8,128)(2,1)}, u32[]{:S(2)}, u32[]{:S(2)}) collective-permute-start(bf16[128,1024]{1,0:T(8,128)(2,1)} %get-tuple-element.78), channel_id=1, source_target_pairs={{0,4},{2,6},{4,0},{6,2},{1,5},{3,7},{5,1},{7,3},{8,12},{10,14},{12... | collective-permute-start | bytes 786440 | tf_op jit(solution)/shard_map/ppermute | solution.py:88
  330.8 28.3 %collective-permute-start.31 = (bf16[128,1024]{1,0:T(8,128)(2,1)}, bf16[128,1024]{1,0:T(8,128)(2,1)}, u32[]{:S(2)}, u32[]{:S(2)}) collective-permute-start(bf16[128,1024]{1,0:T(8,128)(2,1)} %get-tuple-element.76), channel_id=1, source_target_pairs={{0,2},{2,4},{4,6},{6,0},{1,3},{3,5},{5,7},{7,1},{8,10},{10,12},{12... | collective-permute-start | bytes 786440 | tf_op jit(solution)/shard_map/ppermute | solution.py:88
  335.9 24.9 %collective-permute-start.20 = (bf16[128,1024]{1,0:T(8,128)(2,1)}, bf16[128,1024]{1,0:T(8,128)(2,1)}, u32[]{:S(2)}, u32[]{:S(2)}) collective-permute-start(bf16[128,1024]{1,0:T(8,128)(2,1)} %get-tuple-element.85), channel_id=1, source_target_pairs={{0,6},{2,0},{4,2},{6,4},{1,7},{3,1},{5,3},{7,5},{8,14},{10,8},{12,... | collective-permute-start | bytes 786440 | tf_op jit(solution)/shard_map/ppermute | solution.py:88
  338.0 22.8 %collective-permute-start.19 = (bf16[128,1024]{1,0:T(8,128)(2,1)}, bf16[128,1024]{1,0:T(8,128)(2,1)}, u32[]{:S(2)}, u32[]{:S(2)}) collective-permute-start(bf16[128,1024]{1,0:T(8,128)(2,1)} %get-tuple-element.86), channel_id=1, source_target_pairs={{0,4},{2,6},{4,0},{6,2},{1,5},{3,7},{5,1},{7,3},{8,12},{10,14},{12... | collective-permute-start | bytes 786440 | tf_op jit(solution)/shard_map/ppermute | solution.py:88
  348.3 21.8 %all-to-all-start.6 = ((f32[128,1,256]{2,1,0:T(1,128)}), f32[128,1,256]{2,1,0:T(1,128)S(1)}, u32[]{:S(2)}, u32[]{:S(2)}) async-start(f32[128,1,256]{2,1,0:T(1,128)} %broadcast_in_dim.88), calls=%async_computation.6 | async-start | bytes 262144 | tf_op jit(solution)/shard_map/all_to_all | solution.py:678
  357.6 9.4 %collective-permute-start.18 = (bf16[128,1024]{1,0:T(8,128)(2,1)}, bf16[128,1024]{1,0:T(8,128)(2,1)S(1)}, u32[]{:S(2)}, u32[]{:S(2)}) collective-permute-start(bf16[128,1024]{1,0:T(8,128)(2,1)} %get-tuple-element.84), channel_id=1, source_target_pairs={{0,2},{2,4},{4,6},{6,0},{1,3},{3,5},{5,7},{7,1},{8,10},{10,12},{12... | collective-permute-start | bytes 786440 | tf_op jit(solution)/shard_map/ppermute | solution.py:88
  (38 other events, 402.0 us)
